TPU v7x, 32 devices: a whole 2x2x4 slice. The times are simulated.
32 devices in a mesh: groups: 2 (over y), dp: 4 (over z), tensor: 2 (over core), section: 2 (over x).
Axes of the slice: x: 2, y: 2, z: 4, core: 2. Of those that a mesh axis runs over, the one named last changes fastest.
Arguments:
- acts: bfloat16 [2, 1024, 8192], P('section', ('groups', 'dp'), 'tensor'), parts along dimension 1, may hold values from -6 to 6
- grads: bfloat16 [2, 1024, 14336], P('section', ('groups', 'dp'), 'tensor'), parts along dimension 1, may hold values from -6 to 6
- proj_in: bfloat16 [2, 64, 8192], P('section', None, 'tensor'), may hold values from -0.0625 to 0.0625
- proj_out: bfloat16 [2, 64, 14336], P('section', None, 'tensor'), may hold values from -0.046875 to 0.046875
- lengths: int32 [8, 32], P(('groups', 'dp')), parts along dimension 0, may hold values from 1 to 64, 128 in all within a row
- query_ids: int32 [8, 32], P(('groups', 'dp')), parts along dimension 0, may hold values from 0 to 31
- train_logged: bfloat16 [2, 1024, 4096], P('section', ('groups', 'dp')), parts along dimension 1, may hold values from -6 to 6
Outputs:
- scores: float32 [128, 1024], P('section', ('groups', 'dp')), parts along dimension 1
There are 2 independent parts, one for each index of `groups`. A program takes and returns all parts, laid end to end along the dimension named above; an argument that names none is the same for every part. Nothing has to cross between parts.
Inputs may be any that keep to these rules, and one draw needn't show every extreme that they name: Each row of lengths sums to 128; in each row the largest is 64.
All inputs are finite; a program needn't handle non-finite values.
Results may differ from a plain program's by a relative error of at most 0.0029.
Values may be sent and summed in bfloat16 or wider, within the bound.
No kernel may reach another device: no remote copies, remote signals or barrier semaphores. Data moves between devices by JAX's collectives and lax.ppermute only.
A program may use at most 64 MiB of HBM per device.

v0:
```python
import jax
import jax.numpy as jnp
from jax import lax
from jax.sharding import PartitionSpec as P

RANK = 64


def per_device(acts, grads, proj_in, proj_out, lengths, query_ids, train_logged):
    tok_rows = acts.shape[1]
    tok = jnp.arange(tok_rows, dtype=jnp.int32)
    ends = jnp.cumsum(lengths[0])
    seg = jnp.sum((tok[None, :] >= ends[:, None]).astype(jnp.int32), axis=0)
    mask = (seg[None, :] == query_ids[0][:, None]).astype(jnp.float32)
    weighted = mask / jnp.sqrt(jnp.sum(mask, axis=1, keepdims=True))
    xpart = jnp.dot(acts[0], proj_in[0].T, preferred_element_type=jnp.float32)
    gpart = jnp.dot(grads[0], proj_out[0].T, preferred_element_type=jnp.float32)
    logged = train_logged[0]
    summed = lax.psum(jnp.concatenate([gpart, xpart], axis=1), "tensor")
    gproj = summed[:, :RANK]
    xproj = summed[:, RANK:]
    blocks = jnp.einsum("qt,ta,tb->qab", weighted, gproj, xproj, precision=lax.Precision.HIGHEST)
    blocks = blocks.astype(jnp.bfloat16).reshape(blocks.shape[0], blocks.shape[1] * blocks.shape[2])
    partial_scores = jnp.dot(
        lax.all_gather(blocks, "dp", axis=0, tiled=True),
        logged.T,
        preferred_element_type=jnp.float32,
    )
    scores = lax.psum_scatter(partial_scores, "section", scatter_dimension=0, tiled=True)
    return scores / RANK


def solution(mesh):
    in_specs = (
        P("section", ("groups", "dp"), "tensor"),
        P("section", ("groups", "dp"), "tensor"),
        P("section", None, "tensor"),
        P("section", None, "tensor"),
        P(("groups", "dp"), None),
        P(("groups", "dp"), None),
        P("section", ("groups", "dp"), None),
    )
    out_specs = P("section", ("groups", "dp"))
    return jax.shard_map(
        per_device, mesh=mesh, in_specs=in_specs, out_specs=out_specs, check_vma=False
    )
```

profile of v0, /device:TPU:0, one launch (start us, length us, event | category | flops | bytes accessed | tf_op | source)
XLA Modules:
  0.0 84.6 jit_solution(9261993405509888497)
XLA Ops:
  6.5 0.0 copy-start
  6.5 0.0 all-reduce.2.cloned.1.call-start
  6.5 2.0 %fusion.5 = f32[128,64]{0,1:T(8,128)S(1)} fusion(bf16[1,128,4096]{2,1,0:T(8,128)(2,1)} %param.7, bf16[1,64,4096]{2,1,0:T(8,128)(2,1)} %param.9), kind=kOutput, calls=%fused_computation.6 | convolution fusion | flops 67108864 | bytes 1605632 | tf_op jit(solution)/shard_map/dot_general | solution.py:16
  8.5 0.0 copy-done
  8.5 0.0 copy-start.2
  8.5 0.0 copy-start.3
  8.5 1.9 %fusion = f32[128,64]{0,1:T(8,128)S(1)} fusion(bf16[1,128,7168]{2,1,0:T(8,128)(2,1)S(1)} %copy-done, bf16[1,64,7168]{2,1,0:T(8,128)(2,1)} %param.10), kind=kOutput, calls=%fused_computation | convolution fusion | flops 117440512 | bytes 2785280 | tf_op jit(solution)/shard_map/dot_general | solution.py:17
  10.5 0.0 copy-start.1
  10.5 0.6 pad_maximum_fusion
  11.1 0.0 all-reduce.2.cloned.1.call-update
  11.2 0.0 all-gather.2.cloned.1.call-start
  11.2 0.0 copy-done.2
  11.2 0.1 copy.11
  11.3 0.1 reduce-window.8
  11.4 0.1 reduce
  11.5 0.1 convert_reduce_fusion.1
  11.6 0.0 copy-done.3
  11.6 0.2 convert_reduce_fusion
  11.8 0.1 fusion.12
  11.8 19.9 %all-reduce.2.cloned.1.call-done = f32[128,128]{0,1:T(8,128)} async-done(((f32[128,128]{0,1:T(8,128)}), f32[128,128]{0,1:T(8,128)}) %all-reduce.2.cloned.1.call-update) | async-done | bytes 65552 | tf_op jit(solution)/shard_map/psum | solution.py:19
  31.7 0.8 slice.8
  32.5 1.7 %fusion.2 = bf16[32,64,64]{2,0,1:T(8,128)(2,1)S(1)} fusion(f32[128,32]{0,1:T(8,128)S(1)} %fusion.12, f32[128,64]{0,1:T(8,128)S(1)} %slice.8, f32[128,128]{0,1:T(8,128)} %all-reduce.2.cloned.1.call-done), kind=kOutput, calls=%fused_computation.3 | convolution fusion | flops 201719808 | bytes 344064 | tf_op jit(solution)/shard_map/qt,ta,tb->qab/dot_general | solution.py:22
  34.2 0.2 copy.12
  34.4 1.2 %reshape.35 = bf16[32,4096]{1,0:T(8,128)(2,1)} reshape(bf16[32,64,64]{2,1,0:T(8,128)(2,1)S(1)} %copy.12) | data formatting | bytes 524288 | tf_op jit(solution)/shard_map/reshape | solution.py:23
  35.6 0.0 all-gather.2.cloned.1.call-update
  35.6 0.0 reduce-scatter.2.cloned.1.call-start
  35.7 29.2 %all-gather.2.cloned.1.call-done = bf16[128,4096]{1,0:T(8,128)(2,1)} async-done(((bf16[32,4096]{1,0:T(8,128)(2,1)}), bf16[128,4096]{1,0:T(8,128)(2,1)}) %all-gather.2.cloned.1.call-update) | async-done | bytes 1048592 | tf_op jit(solution)/shard_map/all_gather | solution.py:25
  64.9 0.0 copy-done.1
  64.9 2.3 %fusion.3 = f32[128,128]{1,0:T(8,128)} fusion(bf16[128,4096]{1,0:T(8,128)(2,1)} %all-gather.2.cloned.1.call-done, bf16[1,128,4096]{2,1,0:T(8,128)(2,1)S(1)} %copy-done.1), kind=kOutput, calls=%fused_computation.4 | convolution fusion | flops 134217728 | bytes 2162688 | tf_op jit(solution)/shard_map/dot_general | solution.py:24
  67.2 0.0 reduce-scatter.2.cloned.1.call-update
  67.2 9.5 %reduce-scatter.2.cloned.1.call-done = f32[64,128]{1,0:T(8,128)} async-done(((f32[128,128]{1,0:T(8,128)}), f32[64,128]{1,0:T(8,128)}) %reduce-scatter.2.cloned.1.call-update) | async-done | bytes 32784 | tf_op jit(solution)/shard_map/reduce_scatter | solution.py:29
  76.7 1.4 %broadcast_multiply_fusion = f32[64,128]{1,0:T(8,128)} fusion(f32[64,128]{1,0:T(8,128)} %reduce-scatter.2.cloned.1.call-done), kind=kLoop, calls=%fused_computation.18 | loop fusion | flops 8192 | bytes 65536 | tf_op jit(solution)/shard_map/div | solution.py:30
  (1 shorter events, 0.0 us)
Async XLA Ops:
  6.5 2.0 %copy-start = (bf16[1,128,7168]{2,1,0:T(8,128)(2,1)S(1)}, bf16[1,128,7168]{2,1,0:T(8,128)(2,1)}, u32[]{:S(2)}) copy-start(bf16[1,128,7168]{2,1,0:T(8,128)(2,1)} %param.8) | copy-start | bytes 5505028
  6.5 25.2 %all-reduce.2.cloned.1.call-start = ((), (), s32[]{:S(2)}) async-start(), calls=%async_computation.1 | async-start | bytes 131072 | tf_op jit(solution)/shard_map/psum | solution.py:19
  8.5 2.7 %copy-start.2 = (s32[1,32]{1,0:T(1,128)S(1)}, s32[1,32]{1,0:T(1,128)}, u32[]{:S(2)}) copy-start(s32[1,32]{1,0:T(1,128)} %param.11) | copy-start | bytes 388
  8.5 3.0 %copy-start.3 = (s32[1,32]{1,0:T(1,128)S(1)}, s32[1,32]{1,0:T(1,128)}, u32[]{:S(2)}) copy-start(s32[1,32]{1,0:T(1,128)} %param.12) | copy-start | bytes 388
  10.5 54.4 %copy-start.1 = (bf16[1,128,4096]{2,1,0:T(8,128)(2,1)S(1)}, bf16[1,128,4096]{2,1,0:T(8,128)(2,1)}, u32[]{:S(2)}) copy-start(bf16[1,128,4096]{2,1,0:T(8,128)(2,1)} %param.13) | copy-start | bytes 3145732
  11.2 53.7 %all-gather.2.cloned.1.call-start = ((), (), s32[]{:S(2)}) async-start(), calls=%async_computation.2 | async-start | bytes 1310720 | tf_op jit(solution)/shard_map/all_gather | solution.py:25
  35.6 41.1 %reduce-scatter.2.cloned.1.call-start = ((), (), s32[]{:S(2)}) async-start(), calls=%async_computation.3 | async-start | bytes 98304 | tf_op jit(solution)/shard_map/reduce_scatter | solution.py:29
Sparse Core Ops, SparseCore 0:
  11.3 20.3 all-reduce.1
  35.7 29.0 all-gather.1
  67.3 9.3 reduce-scatter.1
where the time goes:
time: 85 us; the launch traced here: 84.6 us
  waiting for transfers between devices  58.7 us (69%)
  between operations  13.2 us (16%)
  matrix products  7.91 us (9%)
  other arithmetic  2.51 us (3%)
  local copies, waits for them, and re-layouts  2.27 us (3%)
    all_gather x1, waiting for transfers between devices, per_device(): lax.all_gather(blocks, 'dp', axis=0, tiled=True)  29.2 us
    psum x1, waiting for transfers between devices, per_device(): summed = lax.psum(jnp.concatenate([gpart, xpart], axis=1), 'tensor')  19.9 us
    reduce_scatter x1, waiting for transfers between devices, per_device(): lax.psum_scatter(partial_scores, 'section', scatter_dimension=0, tiled=True)  9.54 us
    dot_general x1, matrix products, per_device(): jnp.dot(lax.all_gather(blocks, 'dp', axis=0, tiled=True), logged.T, prefe...  2.28 us
    dot_general x1, matrix products, per_device(): xpart = jnp.dot(acts[0], proj_in[0].T, preferred_element_type=jnp.float32)  1.97 us
    dot_general x1, matrix products, per_device(): gpart = jnp.dot(grads[0], proj_out[0].T, preferred_element_type=jnp.float32)  1.93 us
    dot_general x1, matrix products, per_device(): jnp.einsum('qt,ta,tb->qab', weighted, gproj, xproj, precision=lax.Precisi...  1.73 us
  transfers between devices with their start and end apart: 3, of which 3 were waited for; matrix products, arithmetic and copies ran while one was open for 1% of the time, Pallas kernels for 0%

commit v1 on v0

v1 whole, which is shorter than its diff:
```python
import functools

import jax
import jax.numpy as jnp
from jax import lax
from jax.experimental import pallas as pl
from jax.experimental.pallas import tpu as pltpu
from jax.sharding import PartitionSpec as P

RANK = 64
LANES = 128
EXTRA = 8
MIB = 1 << 20
NT = (((1,), (1,)), ((), ()))
VMEM = pl.BlockSpec(memory_space=pltpu.VMEM)


def _nt(a, b):
    return lax.dot_general(a, b, NT, preferred_element_type=jnp.float32)


def _cuts(width, parts):
    edges = [width * sum(parts[:i]) // sum(parts) // LANES * LANES for i in range(len(parts))] + [width]
    return list(zip(edges[:-1], edges[1:]))


ACT_PARTS = (1,)
GRAD_PARTS = (7, 5, 2)


def _project_kernel(acts, grads, pin, pout, out, av, gv, piv, pov, sem):
    steps = []
    for big, small, big_v, small_v, parts, row in ((acts, pin, av, piv, ACT_PARTS, RANK), (grads, pout, gv, pov, GRAD_PARTS, 0)):
        for lo, hi in _cuts(big.shape[1], parts):
            cols = pl.ds(lo, hi - lo)
            i = 2 * len(steps)
            pair = (
                pltpu.make_async_copy(small.at[:, cols], small_v.at[:, cols], sem.at[i]),
                pltpu.make_async_copy(big.at[:, cols], big_v.at[:, cols], sem.at[i + 1]),
            )
            for c in pair:
                c.start()
            steps.append((pair, big_v, small_v, cols, row))
    sums = {}
    for pair, big_v, small_v, cols, row in steps:
        for c in pair:
            c.wait()
        part = _nt(small_v[:, cols], big_v[:, cols])
        sums[row] = sums[row] + part if row in sums else part
    for row, value in sums.items():
        out[row : row + RANK, :] = value


def project(acts, grads, pin, pout):
    args = (acts, grads, pin, pout)
    return pl.pallas_call(
        _project_kernel,
        out_shape=jax.ShapeDtypeStruct((2 * RANK, acts.shape[0]), jnp.float32),
        in_specs=[pl.BlockSpec(memory_space=pl.ANY)] * 4,
        out_specs=VMEM,
        scratch_shapes=[pltpu.VMEM(a.shape, a.dtype) for a in args]
        + [pltpu.SemaphoreType.DMA((2 * (len(ACT_PARTS) + len(GRAD_PARTS)),))],
        compiler_params=pltpu.CompilerParams(vmem_limit_bytes=int(53.7 * MIB)),
        name="project",
    )(*args)


def _tags_kernel(lengths, query_ids, out):
    examples, queries, tokens = lengths.shape[1], query_ids.shape[1], out.shape[1]
    length = jnp.broadcast_to(lengths[...].astype(jnp.float32), (examples, examples))
    row = lax.broadcasted_iota(jnp.int32, (examples, examples), 0)
    col = lax.broadcasted_iota(jnp.int32, (examples, examples), 1)
    ends = jnp.sum(jnp.where(col <= row, length, 0.0), axis=1, keepdims=True)
    tok = lax.broadcasted_iota(jnp.int32, (examples, tokens), 1).astype(jnp.float32)
    out[...] = jnp.zeros_like(out)
    out[0:1, :] = jnp.sum(jnp.where(tok >= ends, 1.0, 0.0), axis=0, keepdims=True)
    out[1:2, :queries] = query_ids[...].astype(jnp.float32)


def tags(lengths, query_ids, tokens):
    return pl.pallas_call(
        _tags_kernel,
        out_shape=jax.ShapeDtypeStruct((EXTRA, tokens), jnp.float32),
        in_specs=[VMEM] * 2,
        out_specs=VMEM,
        compiler_params=pltpu.CompilerParams(vmem_limit_bytes=16 * MIB),
        name="tags",
    )(lengths, query_ids)


def _unit(unit, train, queries):
    tokens = unit.shape[1]
    seg = jnp.broadcast_to(unit[2 * RANK : 2 * RANK + 1, :], (queries, tokens))
    ids = jnp.broadcast_to(unit[2 * RANK + 1 : 2 * RANK + 2, :queries], (queries, queries))
    row = lax.broadcasted_iota(jnp.int32, (queries, queries), 0)
    col = lax.broadcasted_iota(jnp.int32, (queries, queries), 1)
    wanted = jnp.sum(jnp.where(row == col, ids, 0.0), axis=1, keepdims=True)
    mask = jnp.where(seg == wanted, 1.0, 0.0)
    scale = 1.0 / jnp.sqrt(jnp.sum(mask, axis=1, keepdims=True))
    mask = mask.astype(jnp.bfloat16)
    g = unit[0:RANK, :]
    x = unit[RANK : 2 * RANK, :]
    g_hi = g.astype(jnp.bfloat16).astype(jnp.float32)
    g_lo = g - g_hi
    x_hi = x.astype(jnp.bfloat16)
    x_lo = (x - x_hi.astype(jnp.float32)).astype(jnp.bfloat16)
    zero = jnp.zeros_like(x_hi)

    def twice(v):
        return jnp.concatenate([jnp.concatenate([v, zero], axis=1), jnp.concatenate([zero, v], axis=1)], axis=0)

    def masked(v):
        rows = []
        for a in range(0, RANK, 2):
            rows.append(
                jnp.concatenate(
                    [jnp.broadcast_to(v[i : i + 1, :], (queries, tokens)).astype(jnp.bfloat16) * mask for i in (a, a + 1)],
                    axis=1,
                )
            )
        return jnp.concatenate(rows, axis=0)

    x_hi, x_lo = twice(x_hi), twice(x_lo)
    left = masked(g_hi)
    blocks = _nt(left, x_hi) + _nt(left, x_lo) + _nt(masked(g_lo), x_hi)
    blocks = jnp.concatenate(
        [(blocks[i * queries : (i + 1) * queries, :] * scale).astype(jnp.bfloat16) for i in range(RANK // 2)], axis=1
    )
    return _nt(blocks, train[...]) * (1.0 / RANK)


def _scores_kernel(queries, step, keep, sections, per, unit, train, *refs):
    out = refs[-1]
    out[...] = refs[0][...] if len(refs) > 1 else jnp.zeros_like(out)
    mine = tuple(step) if isinstance(step, tuple) else (step, step)

    def add(k):
        other = lax.axis_index("dp") ^ k
        row = ((other // per) ^ lax.axis_index("section")) * per + other % per
        out[pl.ds(pl.multiple_of(row * queries, queries), queries), :] = _unit(unit, train, queries)

    core = lax.axis_index("tensor")
    if keep == (True, True):
        add(jnp.where(core == 0, mine[0], mine[1]))
    else:
        c = keep.index(True)
        pl.when(core == c)(lambda: add(mine[c]))


def scores_of(unit, train, queries, step, keep, sections, n_dp, held=None):
    more = () if held is None else (held,)
    return pl.pallas_call(
        functools.partial(_scores_kernel, queries, step, keep, sections, n_dp // sections),
        out_shape=jax.ShapeDtypeStruct((n_dp * queries, train.shape[0]), jnp.float32),
        in_specs=[VMEM] * (2 + len(more)),
        out_specs=VMEM,
        compiler_params=pltpu.CompilerParams(vmem_limit_bytes=16 * MIB),
        name="scores",
    )(unit, train, *more)


def solution(mesh):
    n_dp, cores, sections = mesh.shape["dp"], mesh.shape["tensor"], mesh.shape["section"]

    def swap(v):
        return lax.ppermute(v, "tensor", [(0, 1), (1, 0)])

    def hand(v, steps):
        return lax.ppermute(
            v, ("dp", "tensor"), [(d * cores + t, (d ^ steps[t]) * cores + t) for d in range(n_dp) for t in range(cores)]
        )

    def per_device(acts, grads, proj_in, proj_out, lengths, query_ids, train_logged):
        train, queries = train_logged[0], query_ids.shape[1]
        part = project(acts[0], grads[0], proj_in[0], proj_out[0])
        marks = tags(lengths, query_ids, part.shape[1])
        own = jnp.concatenate([part + swap(part), marks], axis=0)
        rounds = [(2 * j, 2 * j + 1) for j in range(1, n_dp // 2)] + [(1, 1)]
        units = [hand(own, steps) for steps in rounds]
        total = scores_of(own, train, queries, 0, (False, True), sections, n_dp)
        for steps, unit in zip(rounds, units):
            keep = (steps[0] != steps[1], True)
            total = scores_of(unit, train, queries, steps, keep, sections, n_dp, total)
        rows = total.shape[0] // sections
        kept = total[:rows]
        for k in range(1, sections):
            kept = kept + lax.ppermute(total[k * rows : (k + 1) * rows], "section", [(s, s ^ k) for s in range(sections)])
        return kept + swap(kept)

    in_specs = (
        P("section", ("groups", "dp"), "tensor"),
        P("section", ("groups", "dp"), "tensor"),
        P("section", None, "tensor"),
        P("section", None, "tensor"),
        P(("groups", "dp"), None),
        P(("groups", "dp"), None),
        P("section", ("groups", "dp"), None),
    )
    return jax.shard_map(
        per_device, mesh=mesh, in_specs=in_specs, out_specs=P("section", ("groups", "dp")), check_vma=False
    )
```

time: 85 us -> 20 us (0.24)
  waiting for transfers between devices: 58.7 us -> 6.76 us
  between operations: 13.2 us -> 0.05 us
  matrix products: 7.91 us -> 0 us
  starting transfers between devices: 0.09 us -> 7.77 us
  Pallas kernels: 0 us -> 4.58 us
  local copies, waits for them, and re-layouts: 2.27 us -> 0.02 us
  other arithmetic: 2.51 us -> 0.64 us
    all_gather x1 -> x0, waiting for transfers between devices: 29.2 us -> none  [per_device(): lax.all_gather(blocks, 'dp', axis=0, tiled=True)]
    psum x1 -> x0, waiting for transfers between devices: 19.9 us -> none  [per_device(): summed = lax.psum(jnp.concatenate([gpart, xpart], axis=1), 'tensor')]
    reduce_scatter x1 -> x0, waiting for transfers between devices: 9.54 us -> none  [per_device(): lax.psum_scatter(partial_scores, 'section', scatter_dimension=0, tiled=True)]
    dot_general x4 -> x0, matrix products: 7.91 us -> none  [the longest x1 2.28 us: per_device(): jnp.dot(lax.all_gather(blocks, 'dp', axis=0, tiled=True), logged.T, prefe...]
    ppermute x0 -> x5, starting transfers between devices: none -> 7.77 us  [the longest x2 5.58 us: hand(): lax.ppermute(v, ('dp', 'tensor'), [(d * cores + t, (d ^ steps[t]) * cores...]
    ppermute x0 -> x5, waiting for transfers between devices: none -> 6.76 us  [the longest x1 2.48 us: per_device(): lax.ppermute(total[k * rows:(k + 1) * rows], 'section', [(s, s ^ k) for s...]
    pallas_call x0 -> x5, Pallas kernels: none -> 4.58 us  [the longest x1 3.22 us: project(): pl.pallas_call(_project_kernel, out_shape=jax.ShapeDtypeStruct((2 * RANK,...]
    div x2 -> x0, other arithmetic: 1.45 us -> none  [the longest x1 1.37 us: per_device(): return scores / RANK]
  transfers between devices with their start and end apart: 3 -> 5, of which waited for: 3 -> 4; matrix products, arithmetic and copies ran while one was open for 1% -> 0% of each run, Pallas kernels for 0% -> 7%
where the time goes in v1:
time: 20 us; the launch traced here: 19.8 us
  starting transfers between devices  7.77 us (39%)
  waiting for transfers between devices  6.76 us (34%)
  Pallas kernels  4.58 us (23%)
  other arithmetic  0.64 us (3%)
    ppermute x2, starting transfers between devices, hand(): lax.ppermute(v, ('dp', 'tensor'), [(d * cores + t, (d ^ steps[t]) * cores...  5.58 us
    pallas_call x1, Pallas kernels, project(): pl.pallas_call(_project_kernel, out_shape=jax.ShapeDtypeStruct((2 * RANK,...  3.22 us
    ppermute x1, waiting for transfers between devices, per_device(): lax.ppermute(total[k * rows:(k + 1) * rows], 'section', [(s, s ^ k) for s...  2.48 us
    ppermute x2, waiting for transfers between devices, hand(): lax.ppermute(v, ('dp', 'tensor'), [(d * cores + t, (d ^ steps[t]) * cores...  2.38 us
    ppermute x2, waiting for transfers between devices, swap(): return lax.ppermute(v, 'tensor', [(0, 1), (1, 0)])  1.9 us
    ppermute x1, starting transfers between devices, per_device(): lax.ppermute(total[k * rows:(k + 1) * rows], 'section', [(s, s ^ k) for s...  1.55 us
    pallas_call x3, Pallas kernels, scores_of(): pl.pallas_call(functools.partial(_scores_kernel, queries, step, keep, sec...  1.27 us
    ppermute x2, starting transfers between devices, swap(): return lax.ppermute(v, 'tensor', [(0, 1), (1, 0)])  0.64 us
  transfers between devices with their start and end apart: 5, of which 4 were waited for; matrix products, arithmetic and copies ran while one was open for 0% of the time, Pallas kernels for 7%

profile of v1, /device:TPU:0, one launch (start us, length us, event | category | flops | bytes accessed | tf_op | source)
XLA Modules:
  0.0 19.8 jit_solution(8189771134737348596)
XLA Ops:
  0.0 0.0 copy-start.1
  0.0 0.0 copy-start.2
  0.0 0.0 copy-start
  0.0 3.2 %project.1 = f32[128,128]{1,0:T(8,128)S(1)} custom-call(bf16[128,4096]{1,0:T(8,128)(2,1)} %bitcast.9, bf16[128,7168]{1,0:T(8,128)(2,1)} %bitcast.8, bf16[64,4096]{1,0:T(8,128)(2,1)} %bitcast.11, bf16[64,7168]{1,0:T(8,128)(2,1)} %bitcast.10), custom_call_target="tpu_custom_call" | custom-call | tf_op jit(solution)/shard_map/project/pallas_call | solution.py:56
  3.2 0.5 %collective-permute-start = (f32[128,128]{1,0:T(8,128)S(1)}, f32[128,128]{1,0:T(8,128)S(1)}, u32[]{:S(2)}, u32[]{:S(2)}) collective-permute-start(f32[128,128]{1,0:T(8,128)S(1)} %project.1), channel_id=1, source_target_pairs={{0,2},{2,0},{1,3},{3,1},{4,6},{6,4},{5,7},{7,5},{8,10},{10,8},{9,1... | collective-permute-start | bytes 196616 | tf_op jit(solution)/shard_map/ppermute | solution.py:166
  3.8 0.0 copy-done.1
  3.8 0.0 copy-done.2
  3.8 0.1 tags.1
  3.9 0.8 %collective-permute-done = f32[128,128]{1,0:T(8,128)S(1)} collective-permute-done((f32[128,128]{1,0:T(8,128)S(1)}, f32[128,128]{1,0:T(8,128)S(1)}, u32[]{:S(2)}, u32[]{:S(2)}) %collective-permute-start) | collective-permute-done | bytes 65568 | tf_op jit(solution)/shard_map/ppermute | solution.py:166
  4.7 4.0 %collective-permute-start.2 = (f32[136,128]{1,0:T(8,128)S(1)}, f32[136,128]{1,0:T(8,128)S(1)}, u32[]{:S(2)}, u32[]{:S(2)}) collective-permute-start(f32[136,128]{1,0:T(8,128)S(1)} %pad_maximum_fusion.unit), channel_id=1, source_target_pairs={{0,8},{2,14},{4,12},{6,10},{8,0},{10,6},{12,4},{14,2},{1,9},{3,15}... | collective-permute-start | bytes 208904 | tf_op jit(solution)/shard_map/ppermute | solution.py:169
  8.7 1.6 %collective-permute-start.1 = (f32[136,128]{1,0:T(8,128)S(1)}, f32[136,128]{1,0:T(8,128)S(1)}, u32[]{:S(2)}, u32[]{:S(2)}) collective-permute-start(f32[136,128]{1,0:T(8,128)S(1)} %pad_maximum_fusion.unit), channel_id=1, source_target_pairs={{0,4},{2,6},{4,0},{6,2},{8,12},{10,14},{12,8},{14,10},{1,5},{3,7},... | collective-permute-start | bytes 208904 | tf_op jit(solution)/shard_map/ppermute | solution.py:169
  10.3 0.0 copy-done
  10.3 2.4 %collective-permute-done.2.unit = f32[136,128]{1,0:T(8,128)S(1)} collective-permute-done((f32[136,128]{1,0:T(8,128)S(1)}, f32[136,128]{1,0:T(8,128)S(1)}, u32[]{:S(2)}, u32[]{:S(2)}) %collective-permute-start.2) | collective-permute-done | bytes 69664 | tf_op jit(solution)/shard_map/ppermute | solution.py:169
  12.7 1.2 %scores.4.refs_0_ = f32[128,128]{1,0:T(8,128)S(1)} custom-call(f32[136,128]{1,0:T(8,128)S(1)} %collective-permute-done.2.unit, bf16[128,4096]{1,0:T(8,128)(2,1)S(1)} %bitcast.6, f32[128,128]{1,0:T(8,128)S(1)} %scores.3.refs_0_), custom_call_target="tpu_custom_call" | custom-call | tf_op jit(solution)/shard_map/scores/pallas_call | solution.py:152
  13.9 0.0 collective-permute-done.1.unit
  13.9 1.6 %collective-permute-start.3 = (f32[64,128]{1,0:T(8,128)S(1)}, f32[64,128]{1,0:T(8,128)S(1)}, u32[]{:S(2)}, u32[]{:S(2)}) collective-permute-start(f32[64,128]{1,0:T(8,128)S(1)} %slice.9), channel_id=1, source_target_pairs={{0,1},{1,0},{2,3},{3,2},{4,5},{5,4},{6,7},{7,6},{8,9},{9,8},{10,11... | collective-permute-start | bytes 98312 | tf_op jit(solution)/shard_map/ppermute | solution.py:187
  15.5 2.5 %collective-permute-done.3 = f32[64,128]{1,0:T(8,128)S(1)} collective-permute-done((f32[64,128]{1,0:T(8,128)S(1)}, f32[64,128]{1,0:T(8,128)S(1)}, u32[]{:S(2)}, u32[]{:S(2)}) %collective-permute-start.3) | collective-permute-done | bytes 32800 | tf_op jit(solution)/shard_map/ppermute | solution.py:187
  18.0 0.1 collective-permute-start.4
  18.1 1.1 %collective-permute-done.4 = f32[64,128]{1,0:T(8,128)S(1)} collective-permute-done((f32[64,128]{1,0:T(8,128)S(1)}, f32[64,128]{1,0:T(8,128)S(1)}, u32[]{:S(2)}, u32[]{:S(2)}) %collective-permute-start.4) | collective-permute-done | bytes 32800 | tf_op jit(solution)/shard_map/ppermute | solution.py:166
  19.2 0.6 %add.11 = f32[64,128]{1,0:T(8,128)} add(f32[64,128]{1,0:T(8,128)S(1)} %slice_add_fusion, f32[64,128]{1,0:T(8,128)S(1)} %collective-permute-done.4) | non-fusion elementwise | flops 8192 | bytes 98304 | tf_op jit(solution)/shard_map/add | solution.py:188
  (6 shorter events, 0.1 us)
Async XLA Ops:
  0.0 3.8 %copy-start.1 = (s32[1,32]{1,0:T(1,128)S(1)}, s32[1,32]{1,0:T(1,128)}, u32[]{:S(2)}) copy-start(s32[1,32]{1,0:T(1,128)} %lengths.1) | copy-start | bytes 388
  0.0 3.8 %copy-start.2 = (s32[1,32]{1,0:T(1,128)S(1)}, s32[1,32]{1,0:T(1,128)}, u32[]{:S(2)}) copy-start(s32[1,32]{1,0:T(1,128)} %query_ids.1) | copy-start | bytes 388
  0.0 10.3 %copy-start = (bf16[1,128,4096]{2,1,0:T(8,128)(2,1)S(1)}, bf16[1,128,4096]{2,1,0:T(8,128)(2,1)}, u32[]{:S(2)}) copy-start(bf16[1,128,4096]{2,1,0:T(8,128)(2,1)} %param.13) | copy-start | bytes 3145732
  3.2 1.4 %collective-permute-start = (f32[128,128]{1,0:T(8,128)S(1)}, f32[128,128]{1,0:T(8,128)S(1)}, u32[]{:S(2)}, u32[]{:S(2)}) collective-permute-start(f32[128,128]{1,0:T(8,128)S(1)} %project.1), channel_id=1, source_target_pairs={{0,2},{2,0},{1,3},{3,1},{4,6},{6,4},{5,7},{7,5},{8,10},{10,8},{9,1... | collective-permute-start | bytes 196616 | tf_op jit(solution)/shard_map/ppermute | solution.py:166
  4.7 8.0 %collective-permute-start.2 = (f32[136,128]{1,0:T(8,128)S(1)}, f32[136,128]{1,0:T(8,128)S(1)}, u32[]{:S(2)}, u32[]{:S(2)}) collective-permute-start(f32[136,128]{1,0:T(8,128)S(1)} %pad_maximum_fusion.unit), channel_id=1, source_target_pairs={{0,8},{2,14},{4,12},{6,10},{8,0},{10,6},{12,4},{14,2},{1,9},{3,15}... | collective-permute-start | bytes 208904 | tf_op jit(solution)/shard_map/ppermute | solution.py:169
  8.7 5.2 %collective-permute-start.1 = (f32[136,128]{1,0:T(8,128)S(1)}, f32[136,128]{1,0:T(8,128)S(1)}, u32[]{:S(2)}, u32[]{:S(2)}) collective-permute-start(f32[136,128]{1,0:T(8,128)S(1)} %pad_maximum_fusion.unit), channel_id=1, source_target_pairs={{0,4},{2,6},{4,0},{6,2},{8,12},{10,14},{12,8},{14,10},{1,5},{3,7},... | collective-permute-start | bytes 208904 | tf_op jit(solution)/shard_map/ppermute | solution.py:169
  13.9 4.0 %collective-permute-start.3 = (f32[64,128]{1,0:T(8,128)S(1)}, f32[64,128]{1,0:T(8,128)S(1)}, u32[]{:S(2)}, u32[]{:S(2)}) collective-permute-start(f32[64,128]{1,0:T(8,128)S(1)} %slice.9), channel_id=1, source_target_pairs={{0,1},{1,0},{2,3},{3,2},{4,5},{5,4},{6,7},{7,6},{8,9},{9,8},{10,11... | collective-permute-start | bytes 98312 | tf_op jit(solution)/shard_map/ppermute | solution.py:187
  18.0 1.2 %collective-permute-start.4 = (f32[64,128]{1,0:T(8,128)S(1)}, f32[64,128]{1,0:T(8,128)S(1)}, u32[]{:S(2)}, u32[]{:S(2)}) collective-permute-start(f32[64,128]{1,0:T(8,128)S(1)} %slice_add_fusion), channel_id=1, source_target_pairs={{0,2},{2,0},{1,3},{3,1},{4,6},{6,4},{5,7},{7,5},{8,10},{10,8},{9,1... | collective-permute-start | bytes 98312 | tf_op jit(solution)/shard_map/ppermute | solution.py:166

commit v2 on v1

--- a/solution.py
+++ b/solution.py
@@ -9,7 +9,10 @@
 
 RANK = 64
 LANES = 128
-EXTRA = 8
+EXTRA = 16
+LEVEL = 2.0**16
+LEVELS = 7
+CHUNK = 8
 MIB = 1 << 20
 NT = (((1,), (1,)), ((), ()))
 VMEM = pl.BlockSpec(memory_space=pltpu.VMEM)
@@ -88,7 +91,48 @@
     )(lengths, query_ids)
 
 
-def _unit(unit, train, queries):
+def _pack_kernel(mine, other, marks, out):
+    out[2 * RANK :, :] = marks[...]
+    for i in range(2):
+        rows = pl.ds(i * RANK, RANK)
+        value = mine[rows, :] + other[rows, :]
+        peak = jnp.max(jnp.abs(value), axis=0, keepdims=True)
+        scale, level = jnp.ones_like(peak), jnp.zeros_like(peak)
+        for _ in range(LEVELS):
+            low = peak * scale < 0.5
+            scale = jnp.where(low, scale * LEVEL, scale)
+            level = jnp.where(low, level + 1.0, level)
+        out[rows, :] = value * scale
+        out[2 * RANK + 2 + i : 2 * RANK + 3 + i, :] = level
+
+
+def pack(mine, other, marks):
+    return pl.pallas_call(
+        _pack_kernel,
+        out_shape=jax.ShapeDtypeStruct((2 * RANK + EXTRA, mine.shape[1]), jnp.float32),
+        in_specs=[VMEM] * 3,
+        out_specs=VMEM,
+        compiler_params=pltpu.CompilerParams(vmem_limit_bytes=16 * MIB),
+        name="pack",
+    )(mine, other, marks)
+
+
+def _turn_kernel(rows, out):
+    out[...] = rows[...].T
+
+
+def turn(rows):
+    return pl.pallas_call(
+        _turn_kernel,
+        out_shape=jax.ShapeDtypeStruct(rows.shape[::-1], rows.dtype),
+        in_specs=[VMEM],
+        out_specs=VMEM,
+        compiler_params=pltpu.CompilerParams(vmem_limit_bytes=16 * MIB),
+        name="turn",
+    )(rows)
+
+
+def _unit(unit, train, queries, first=0, last=RANK):
     tokens = unit.shape[1]
     seg = jnp.broadcast_to(unit[2 * RANK : 2 * RANK + 1, :], (queries, tokens))
     ids = jnp.broadcast_to(unit[2 * RANK + 1 : 2 * RANK + 2, :queries], (queries, queries))
@@ -96,37 +140,37 @@
     col = lax.broadcasted_iota(jnp.int32, (queries, queries), 1)
     wanted = jnp.sum(jnp.where(row == col, ids, 0.0), axis=1, keepdims=True)
     mask = jnp.where(seg == wanted, 1.0, 0.0)
-    scale = 1.0 / jnp.sqrt(jnp.sum(mask, axis=1, keepdims=True))
+    norm = 1.0 / jnp.sqrt(jnp.sum(mask, axis=1, keepdims=True))
     mask = mask.astype(jnp.bfloat16)
-    g = unit[0:RANK, :]
-    x = unit[RANK : 2 * RANK, :]
-    g_hi = g.astype(jnp.bfloat16).astype(jnp.float32)
-    g_lo = g - g_hi
-    x_hi = x.astype(jnp.bfloat16)
-    x_lo = (x - x_hi.astype(jnp.float32)).astype(jnp.bfloat16)
-    zero = jnp.zeros_like(x_hi)
+
+    def side(i):
+        level = unit[2 * RANK + 2 + i : 2 * RANK + 3 + i, :]
+        scale = jnp.ones_like(level)
+        for k in range(LEVELS):
+            scale = scale * jnp.where(level > k, 1.0 / LEVEL, 1.0)
+        value = unit[i * RANK : (i + 1) * RANK, :] * scale
+        high = value.astype(jnp.bfloat16).astype(jnp.float32)
+        return high, value - high
 
     def twice(v):
+        v = v.astype(jnp.bfloat16)
+        zero = jnp.zeros_like(v)
         return jnp.concatenate([jnp.concatenate([v, zero], axis=1), jnp.concatenate([zero, v], axis=1)], axis=0)
 
-    def masked(v):
-        rows = []
-        for a in range(0, RANK, 2):
-            rows.append(
-                jnp.concatenate(
-                    [jnp.broadcast_to(v[i : i + 1, :], (queries, tokens)).astype(jnp.bfloat16) * mask for i in (a, a + 1)],
-                    axis=1,
-                )
-            )
-        return jnp.concatenate(rows, axis=0)
-
-    x_hi, x_lo = twice(x_hi), twice(x_lo)
-    left = masked(g_hi)
-    blocks = _nt(left, x_hi) + _nt(left, x_lo) + _nt(masked(g_lo), x_hi)
-    blocks = jnp.concatenate(
-        [(blocks[i * queries : (i + 1) * queries, :] * scale).astype(jnp.bfloat16) for i in range(RANK // 2)], axis=1
-    )
-    return _nt(blocks, train[...]) * (1.0 / RANK)
+    g, x = side(0), side(1)
+    right = jnp.concatenate([twice(x[0]), twice(x[1])], axis=0)
+    right = jnp.concatenate([right, right], axis=1)
+    blocks = []
+    for lo in range(first, last, 2 * CHUNK):
+        left = []
+        for a in range(lo, min(lo + 2 * CHUNK, last), 2):
+            parts = [jnp.broadcast_to(v[i : i + 1, :], (queries, tokens)).astype(jnp.bfloat16) * mask for v in g for i in (a, a + 1)]
+            left.append(jnp.concatenate(parts, axis=1))
+        both = _nt(jnp.concatenate(left, axis=0), right)
+        both = both[:, : 2 * RANK] + both[:, 2 * RANK :]
+        blocks += [(both[i * queries : (i + 1) * queries, :] * norm).astype(jnp.bfloat16) for i in range(len(left))]
+    blocks = jnp.concatenate(blocks, axis=1)
+    return jnp.dot(blocks, train[first * RANK : last * RANK, :], preferred_element_type=jnp.float32) * (1.0 / RANK)
 
 
 def _scores_kernel(queries, step, keep, sections, per, unit, train, *refs):
@@ -151,7 +195,7 @@
     more = () if held is None else (held,)
     return pl.pallas_call(
         functools.partial(_scores_kernel, queries, step, keep, sections, n_dp // sections),
-        out_shape=jax.ShapeDtypeStruct((n_dp * queries, train.shape[0]), jnp.float32),
+        out_shape=jax.ShapeDtypeStruct((n_dp * queries, train.shape[1]), jnp.float32),
         in_specs=[VMEM] * (2 + len(more)),
         out_specs=VMEM,
         compiler_params=pltpu.CompilerParams(vmem_limit_bytes=16 * MIB),
@@ -159,6 +203,69 @@
     )(unit, train, *more)
 
 
+def _own_kernel(queries, own, train, out):
+    @pl.when(lax.axis_index("tensor") == 0)
+    def _():
+        out[...] = _unit(own, train, queries)
+
+    @pl.when(lax.axis_index("tensor") != 0)
+    def _():
+        out[...] = jnp.zeros_like(out)
+
+
+def _far_kernel(queries, scored, far, train, out):
+    sent = lax.axis_index("dp") // 2 == lax.axis_index("section")
+
+    @pl.when(sent)
+    def _():
+        out[...] = _unit(far, train, queries)
+
+    @pl.when(jnp.logical_not(sent))
+    def _():
+        out[...] = scored[...]
+
+
+def _sent_kernel(queries, first, near, train, out):
+    sent = lax.axis_index("dp") // 2 == lax.axis_index("section")
+    use_near = jnp.logical_not(sent) & (lax.axis_index("tensor") != 0)
+
+    @pl.when(use_near)
+    def _():
+        out[...] = _unit(near, train, queries)
+
+    @pl.when(jnp.logical_not(use_near))
+    def _():
+        out[...] = first[...]
+
+
+def _kept_kernel(queries, scored, far, near, train, out):
+    sent = lax.axis_index("dp") // 2 == lax.axis_index("section")
+    core = lax.axis_index("tensor")
+
+    @pl.when(jnp.logical_not(sent))
+    def _():
+        out[...] = _unit(far, train, queries)
+
+    @pl.when(sent & (core == 0))
+    def _():
+        out[...] = scored[...]
+
+    @pl.when(sent & (core != 0))
+    def _():
+        out[...] = _unit(near, train, queries)
+
+
+def _score_call(kernel, queries, name, *args):
+    return pl.pallas_call(
+        kernel,
+        out_shape=jax.ShapeDtypeStruct((queries, args[-1].shape[1]), jnp.float32),
+        in_specs=[VMEM] * len(args),
+        out_specs=VMEM,
+        compiler_params=pltpu.CompilerParams(vmem_limit_bytes=16 * MIB),
+        name=name,
+    )(*args)
+
+
 def solution(mesh):
     n_dp, cores, sections = mesh.shape["dp"], mesh.shape["tensor"], mesh.shape["section"]
 
@@ -167,24 +274,46 @@
 
     def hand(v, steps):
         return lax.ppermute(
-            v, ("dp", "tensor"), [(d * cores + t, (d ^ steps[t]) * cores + t) for d in range(n_dp) for t in range(cores)]
+            v,
+            ("dp", "tensor"),
+            [(d * cores + t, (d ^ steps[1 - t]) * cores + 1 - t) for d in range(n_dp) for t in range(cores)],
         )
 
+    def hand_section(v, step):
+        return lax.ppermute(
+            v,
+            ("tensor", "section"),
+            [(t * sections + s, (1 - t) * sections + (s ^ step)) for s in range(sections) for t in range(cores)],
+        )
+
+    def four_by_two(own, train, queries):
+        far, near = (hand(own, steps).astype(jnp.float32) for steps in ((2, 3), (1, 1)))
+        scored = _score_call(functools.partial(_own_kernel, queries), queries, "own", own.astype(jnp.float32), train)
+        first = _score_call(functools.partial(_far_kernel, queries), queries, "far", scored, far, train)
+        sent = _score_call(functools.partial(_sent_kernel, queries), queries, "sent", first, near, train)
+        got = hand_section(sent, 1)
+        kept = _score_call(functools.partial(_kept_kernel, queries), queries, "kept", scored, far, near, train)
+        kept_first = (lax.axis_index("dp") + lax.axis_index("tensor")) % 2 == 0
+        both = jnp.where(kept_first, jnp.concatenate([kept, got]), jnp.concatenate([got, kept]))
+        return both + swap(both)
+
     def per_device(acts, grads, proj_in, proj_out, lengths, query_ids, train_logged):
-        train, queries = train_logged[0], query_ids.shape[1]
+        train, queries = turn(train_logged[0]), query_ids.shape[1]
         part = project(acts[0], grads[0], proj_in[0], proj_out[0])
         marks = tags(lengths, query_ids, part.shape[1])
-        own = jnp.concatenate([part + swap(part), marks], axis=0)
+        own = pack(part, swap(part), marks).astype(jnp.float16)
+        if (n_dp, sections) == (4, 2):
+            return four_by_two(own, train, queries)
         rounds = [(2 * j, 2 * j + 1) for j in range(1, n_dp // 2)] + [(1, 1)]
         units = [hand(own, steps) for steps in rounds]
-        total = scores_of(own, train, queries, 0, (False, True), sections, n_dp)
+        total = scores_of(own.astype(jnp.float32), train, queries, 0, (False, True), sections, n_dp)
         for steps, unit in zip(rounds, units):
             keep = (steps[0] != steps[1], True)
-            total = scores_of(unit, train, queries, steps, keep, sections, n_dp, total)
+            total = scores_of(unit.astype(jnp.float32), train, queries, steps, keep, sections, n_dp, total)
         rows = total.shape[0] // sections
         kept = total[:rows]
         for k in range(1, sections):
-            kept = kept + lax.ppermute(total[k * rows : (k + 1) * rows], "section", [(s, s ^ k) for s in range(sections)])
+            kept = kept + hand_section(total[k * rows : (k + 1) * rows], k)
         return kept + swap(kept)
 
     in_specs = (

time: 20 us -> 18.2 us (0.910)
  waiting for transfers between devices: 6.76 us -> 5.31 us
  starting transfers between devices: 7.77 us -> 7.08 us
  Pallas kernels: 4.58 us -> 4.98 us
    ppermute x3, waiting for transfers between devices: 4.86 us -> 3.42 us  [the longest x1 2.19 us: hand_section(): lax.ppermute(v, ('tensor', 'section'), [(t * sections + s, (1 - t) * sect...]
    ppermute x3, starting transfers between devices: 7.13 us -> 6.44 us  [the longest x2 5.28 us: hand(): lax.ppermute(v, ('dp', 'tensor'), [(d * cores + t, (d ^ steps[1 - t]) * c...]
    pallas_call x3 -> x6, Pallas kernels: 1.27 us -> 1.66 us  [the longest x4 1.3 us: _score_call(): pl.pallas_call(kernel, out_shape=jax.ShapeDtypeStruct((queries, args[-1]....]
    add x3 -> x1, other arithmetic: 0.63 us -> 0.62 us  [four_by_two(): return both + swap(both)]
  transfers between devices with their start and end apart: 5 -> 5, of which waited for: 4 -> 5; matrix products, arithmetic and copies ran while one was open for 0% -> 0% of each run, Pallas kernels for 7% -> 9%
where the time goes in v2:
time: 18.2 us; the launch traced here: 18.1 us
  starting transfers between devices  7.08 us (39%)
  waiting for transfers between devices  5.31 us (29%)
  Pallas kernels  4.98 us (27%)
  other arithmetic  0.65 us (4%)
    ppermute x2, starting transfers between devices, hand(): lax.ppermute(v, ('dp', 'tensor'), [(d * cores + t, (d ^ steps[1 - t]) * c...  5.28 us
    pallas_call x1, Pallas kernels, project(): pl.pallas_call(_project_kernel, out_shape=jax.ShapeDtypeStruct((2 * RANK,...  3.22 us
    ppermute x1, waiting for transfers between devices, hand_section(): lax.ppermute(v, ('tensor', 'section'), [(t * sections + s, (1 - t) * sect...  2.19 us
    ppermute x2, waiting for transfers between devices, swap(): return lax.ppermute(v, 'tensor', [(0, 1), (1, 0)])  1.9 us
    pallas_call x4, Pallas kernels, _score_call(): pl.pallas_call(kernel, out_shape=jax.ShapeDtypeStruct((queries, args[-1]....  1.3 us
    ppermute x2, waiting for transfers between devices, hand(): lax.ppermute(v, ('dp', 'tensor'), [(d * cores + t, (d ^ steps[1 - t]) * c...  1.23 us
    ppermute x1, starting transfers between devices, hand_section(): lax.ppermute(v, ('tensor', 'section'), [(t * sections + s, (1 - t) * sect...  1.16 us
    ppermute x2, starting transfers between devices, swap(): return lax.ppermute(v, 'tensor', [(0, 1), (1, 0)])  0.64 us
  transfers between devices with their start and end apart: 5, of which 5 were waited for; matrix products, arithmetic and copies ran while one was open for 0% of the time, Pallas kernels for 9%

profile of v2, /device:TPU:0, one launch (start us, length us, event | category | flops | bytes accessed | tf_op | source)
XLA Modules:
  0.0 18.1 jit_solution(10421670385633678533)
XLA Ops:
  0.0 0.0 copy-start.1
  0.0 0.0 copy-start.2
  0.0 0.0 copy-start
  0.0 3.2 %project.1.mine = f32[128,128]{1,0:T(8,128)S(1)} custom-call(bf16[128,4096]{1,0:T(8,128)(2,1)} %bitcast.7, bf16[128,7168]{1,0:T(8,128)(2,1)} %bitcast.6, bf16[64,4096]{1,0:T(8,128)(2,1)} %bitcast.9, bf16[64,7168]{1,0:T(8,128)(2,1)} %bitcast.8), custom_call_target="tpu_custom_call" | custom-call | tf_op jit(solution)/shard_map/project/pallas_call | solution.py:59
  3.2 0.5 %collective-permute-start = (f32[128,128]{1,0:T(8,128)S(1)}, f32[128,128]{1,0:T(8,128)S(1)}, u32[]{:S(2)}, u32[]{:S(2)}) collective-permute-start(f32[128,128]{1,0:T(8,128)S(1)} %project.1.mine), channel_id=1, source_target_pairs={{0,2},{2,0},{1,3},{3,1},{4,6},{6,4},{5,7},{7,5},{8,10},{10,8},{9,1... | collective-permute-start | bytes 196616 | tf_op jit(solution)/shard_map/ppermute | solution.py:273
  3.8 0.0 copy-done.1
  3.8 0.0 copy-done.2
  3.8 0.1 tags.1.marks
  3.9 0.8 %collective-permute-done.other = f32[128,128]{1,0:T(8,128)S(1)} collective-permute-done((f32[128,128]{1,0:T(8,128)S(1)}, f32[128,128]{1,0:T(8,128)S(1)}, u32[]{:S(2)}, u32[]{:S(2)}) %collective-permute-start) | collective-permute-done | bytes 65568 | tf_op jit(solution)/shard_map/ppermute | solution.py:273
  4.7 4.8 %collective-permute-start.1 = (f16[144,128]{1,0:T(8,128)(2,1)S(1)}, f16[144,128]{1,0:T(8,128)(2,1)S(1)}, u32[]{:S(2)}, u32[]{:S(2)}) collective-permute-start(f16[144,128]{1,0:T(8,128)(2,1)S(1)} %get-tuple-element.6), channel_id=1, source_target_pairs={{0,14},{2,8},{4,10},{6,12},{8,6},{10,0},{12,2},{14,4},{1,15},{3,9}... | collective-permute-start | bytes 110600 | tf_op jit(solution)/shard_map/ppermute | solution.py:276
  9.5 0.5 %collective-permute-start.2 = (f16[144,128]{1,0:T(8,128)(2,1)S(1)}, f16[144,128]{1,0:T(8,128)(2,1)S(1)}, u32[]{:S(2)}, u32[]{:S(2)}) collective-permute-start(f16[144,128]{1,0:T(8,128)(2,1)S(1)} %get-tuple-element.6), channel_id=1, source_target_pairs={{0,6},{2,4},{4,2},{6,0},{8,14},{10,12},{12,10},{14,8},{1,7},{3,5},... | collective-permute-start | bytes 110600 | tf_op jit(solution)/shard_map/ppermute | solution.py:276
  10.0 0.0 copy-done
  10.0 0.3 %turn.1.train = bf16[4096,128]{1,0:T(8,128)(2,1)S(1)} custom-call(bf16[128,4096]{1,0:T(8,128)(2,1)S(1)} %bitcast.5), custom_call_target="tpu_custom_call" | custom-call | tf_op jit(solution)/shard_map/turn/pallas_call | solution.py:125
  10.3 0.6 %own.1.scored = f32[32,128]{1,0:T(8,128)S(1)} custom-call(f32[144,128]{1,0:T(8,128)S(1)} %get-tuple-element.5.own, bf16[4096,128]{1,0:T(8,128)(2,1)S(1)} %turn.1.train), custom_call_target="tpu_custom_call" | custom-call | tf_op jit(solution)/shard_map/own/pallas_call | solution.py:259
  11.0 0.1 collective-permute-done.1
  11.1 0.6 %far.1.first = f32[32,128]{1,0:T(8,128)S(1)} custom-call(f32[32,128]{1,0:T(8,128)S(1)} %own.1.scored, f32[144,128]{1,0:T(8,128)S(1)} %convert_element_type.14.far, bf16[4096,128]{1,0:T(8,128)(2,1)S(1)} %turn.1.train), custom_call_target="tpu_custom_call" | custom-call | tf_op jit(solution)/shard_map/far/pallas_call | solution.py:259
  11.8 1.1 %collective-permute-done.2 = f16[144,128]{1,0:T(8,128)(2,1)S(1)} collective-permute-done((f16[144,128]{1,0:T(8,128)(2,1)S(1)}, f16[144,128]{1,0:T(8,128)(2,1)S(1)}, u32[]{:S(2)}, u32[]{:S(2)}) %collective-permute-start.2) | collective-permute-done | bytes 36896 | tf_op jit(solution)/shard_map/ppermute | solution.py:276
  12.9 1.2 %collective-permute-start.3 = (f32[32,128]{1,0:T(8,128)S(1)}, f32[32,128]{1,0:T(8,128)S(1)}, u32[]{:S(2)}, u32[]{:S(2)}) collective-permute-start(f32[32,128]{1,0:T(8,128)S(1)} %sent.1), channel_id=1, source_target_pairs={{0,3},{2,1},{1,2},{3,0},{4,7},{6,5},{5,6},{7,4},{8,11},{10,9},{9,1... | collective-permute-start | bytes 49160 | tf_op jit(solution)/shard_map/ppermute | solution.py:283
  14.1 2.2 %collective-permute-done.3 = f32[32,128]{1,0:T(8,128)S(1)} collective-permute-done((f32[32,128]{1,0:T(8,128)S(1)}, f32[32,128]{1,0:T(8,128)S(1)}, u32[]{:S(2)}, u32[]{:S(2)}) %collective-permute-start.3) | collective-permute-done | bytes 16416 | tf_op jit(solution)/shard_map/ppermute | solution.py:283
  16.3 0.1 collective-permute-start.4
  16.4 1.1 %collective-permute-done.4 = f32[64,128]{1,0:T(8,128)S(1)} collective-permute-done((f32[64,128]{1,0:T(8,128)S(1)}, f32[64,128]{1,0:T(8,128)S(1)}, u32[]{:S(2)}, u32[]{:S(2)}) %collective-permute-start.4) | collective-permute-done | bytes 32800 | tf_op jit(solution)/shard_map/ppermute | solution.py:273
  17.5 0.6 %add.12 = f32[64,128]{1,0:T(8,128)} add(f32[64,128]{1,0:T(8,128)S(1)} %maximum_select_fusion, f32[64,128]{1,0:T(8,128)S(1)} %collective-permute-done.4) | non-fusion elementwise | flops 8192 | bytes 98304 | tf_op jit(solution)/shard_map/add | solution.py:298
  (7 shorter events, 0.1 us)
Async XLA Ops:
  0.0 3.8 %copy-start.1 = (s32[1,32]{1,0:T(1,128)S(1)}, s32[1,32]{1,0:T(1,128)}, u32[]{:S(2)}) copy-start(s32[1,32]{1,0:T(1,128)} %lengths.1) | copy-start | bytes 388
  0.0 3.8 %copy-start.2 = (s32[1,32]{1,0:T(1,128)S(1)}, s32[1,32]{1,0:T(1,128)}, u32[]{:S(2)}) copy-start(s32[1,32]{1,0:T(1,128)} %query_ids.1) | copy-start | bytes 388
  0.0 10.0 %copy-start = (bf16[1,128,4096]{2,1,0:T(8,128)(2,1)S(1)}, bf16[1,128,4096]{2,1,0:T(8,128)(2,1)}, u32[]{:S(2)}) copy-start(bf16[1,128,4096]{2,1,0:T(8,128)(2,1)} %param.13) | copy-start | bytes 3145732
  3.2 1.4 %collective-permute-start = (f32[128,128]{1,0:T(8,128)S(1)}, f32[128,128]{1,0:T(8,128)S(1)}, u32[]{:S(2)}, u32[]{:S(2)}) collective-permute-start(f32[128,128]{1,0:T(8,128)S(1)} %project.1.mine), channel_id=1, source_target_pairs={{0,2},{2,0},{1,3},{3,1},{4,6},{6,4},{5,7},{7,5},{8,10},{10,8},{9,1... | collective-permute-start | bytes 196616 | tf_op jit(solution)/shard_map/ppermute | solution.py:273
  4.7 6.4 %collective-permute-start.1 = (f16[144,128]{1,0:T(8,128)(2,1)S(1)}, f16[144,128]{1,0:T(8,128)(2,1)S(1)}, u32[]{:S(2)}, u32[]{:S(2)}) collective-permute-start(f16[144,128]{1,0:T(8,128)(2,1)S(1)} %get-tuple-element.6), channel_id=1, source_target_pairs={{0,14},{2,8},{4,10},{6,12},{8,6},{10,0},{12,2},{14,4},{1,15},{3,9}... | collective-permute-start | bytes 110600 | tf_op jit(solution)/shard_map/ppermute | solution.py:276
  9.5 3.4 %collective-permute-start.2 = (f16[144,128]{1,0:T(8,128)(2,1)S(1)}, f16[144,128]{1,0:T(8,128)(2,1)S(1)}, u32[]{:S(2)}, u32[]{:S(2)}) collective-permute-start(f16[144,128]{1,0:T(8,128)(2,1)S(1)} %get-tuple-element.6), channel_id=1, source_target_pairs={{0,6},{2,4},{4,2},{6,0},{8,14},{10,12},{12,10},{14,8},{1,7},{3,5},... | collective-permute-start | bytes 110600 | tf_op jit(solution)/shard_map/ppermute | solution.py:276
  12.9 3.4 %collective-permute-start.3 = (f32[32,128]{1,0:T(8,128)S(1)}, f32[32,128]{1,0:T(8,128)S(1)}, u32[]{:S(2)}, u32[]{:S(2)}) collective-permute-start(f32[32,128]{1,0:T(8,128)S(1)} %sent.1), channel_id=1, source_target_pairs={{0,3},{2,1},{1,2},{3,0},{4,7},{6,5},{5,6},{7,4},{8,11},{10,9},{9,1... | collective-permute-start | bytes 49160 | tf_op jit(solution)/shard_map/ppermute | solution.py:283
  16.3 1.2 %collective-permute-start.4 = (f32[64,128]{1,0:T(8,128)S(1)}, f32[64,128]{1,0:T(8,128)S(1)}, u32[]{:S(2)}, u32[]{:S(2)}) collective-permute-start(f32[64,128]{1,0:T(8,128)S(1)} %maximum_select_fusion), channel_id=1, source_target_pairs={{0,2},{2,0},{1,3},{3,1},{4,6},{6,4},{5,7},{7,5},{8,10},{10,8},{9,1... | collective-permute-start | bytes 98312 | tf_op jit(solution)/shard_map/ppermute | solution.py:273

commit v3 on v2

--- a/solution.py
+++ b/solution.py
@@ -9,7 +9,7 @@
 
 RANK = 64
 LANES = 128
-EXTRA = 16
+EXTRA = 8
 LEVEL = 2.0**16
 LEVELS = 7
 CHUNK = 8
@@ -37,10 +37,11 @@
         for lo, hi in _cuts(big.shape[1], parts):
             cols = pl.ds(lo, hi - lo)
             i = 2 * len(steps)
-            pair = (
-                pltpu.make_async_copy(small.at[:, cols], small_v.at[:, cols], sem.at[i]),
-                pltpu.make_async_copy(big.at[:, cols], big_v.at[:, cols], sem.at[i + 1]),
-            )
+            quarter = big.shape[0] // 4
+            pair = [pltpu.make_async_copy(small.at[:, cols], small_v.at[:, cols], sem.at[i])]
+            for r in range(4):
+                rows = pl.ds(r * quarter, quarter)
+                pair.append(pltpu.make_async_copy(big.at[rows, cols], big_v.at[rows, cols], sem.at[i + 1]))
             for c in pair:
                 c.start()
             steps.append((pair, big_v, small_v, cols, row))
@@ -291,7 +292,7 @@
         scored = _score_call(functools.partial(_own_kernel, queries), queries, "own", own.astype(jnp.float32), train)
         first = _score_call(functools.partial(_far_kernel, queries), queries, "far", scored, far, train)
         sent = _score_call(functools.partial(_sent_kernel, queries), queries, "sent", first, near, train)
-        got = hand_section(sent, 1)
+        got = hand_section(sent.astype(jnp.bfloat16), 1).astype(jnp.float32)
         kept = _score_call(functools.partial(_kept_kernel, queries), queries, "kept", scored, far, near, train)
         kept_first = (lax.axis_index("dp") + lax.axis_index("tensor")) % 2 == 0
         both = jnp.where(kept_first, jnp.concatenate([kept, got]), jnp.concatenate([got, kept]))

time: 18.2 us -> 18.1 us (level)
  no operation moved by 1% of the time
where the time goes in v3:
time: 18.1 us; the launch traced here: 18 us
  starting transfers between devices  7.12 us (39%)
  waiting for transfers between devices  5.16 us (29%)
  Pallas kernels  4.94 us (27%)
  other arithmetic  0.66 us (4%)
    ppermute x2, starting transfers between devices, hand(): lax.ppermute(v, ('dp', 'tensor'), [(d * cores + t, (d ^ steps[1 - t]) * c...  5.29 us
    pallas_call x1, Pallas kernels, project(): pl.pallas_call(_project_kernel, out_shape=jax.ShapeDtypeStruct((2 * RANK,...  3.19 us
    ppermute x1, waiting for transfers between devices, hand_section(): lax.ppermute(v, ('tensor', 'section'), [(t * sections + s, (1 - t) * sect...  2.05 us
    ppermute x2, waiting for transfers between devices, swap(): return lax.ppermute(v, 'tensor', [(0, 1), (1, 0)])  1.9 us
    pallas_call x4, Pallas kernels, _score_call(): pl.pallas_call(kernel, out_shape=jax.ShapeDtypeStruct((queries, args[-1]....  1.3 us
    ppermute x2, waiting for transfers between devices, hand(): lax.ppermute(v, ('dp', 'tensor'), [(d * cores + t, (d ^ steps[1 - t]) * c...  1.21 us
    ppermute x1, starting transfers between devices, hand_section(): lax.ppermute(v, ('tensor', 'section'), [(t * sections + s, (1 - t) * sect...  1.13 us
    ppermute x2, starting transfers between devices, swap(): return lax.ppermute(v, 'tensor', [(0, 1), (1, 0)])  0.7 us
  transfers between devices with their start and end apart: 5, of which 5 were waited for; matrix products, arithmetic and copies ran while one was open for 0% of the time, Pallas kernels for 9%

profile of v3, /device:TPU:0, one launch (start us, length us, event | category | flops | bytes accessed | tf_op | source)
XLA Modules:
  0.0 18.0 jit_solution(10877599705461361152)
XLA Ops:
  0.0 0.0 copy-start.1
  0.0 0.0 copy-start.2
  0.0 0.0 copy-start
  0.0 3.2 %project.1.mine = f32[128,128]{1,0:T(8,128)S(1)} custom-call(bf16[128,4096]{1,0:T(8,128)(2,1)} %bitcast.7, bf16[128,7168]{1,0:T(8,128)(2,1)} %bitcast.6, bf16[64,4096]{1,0:T(8,128)(2,1)} %bitcast.9, bf16[64,7168]{1,0:T(8,128)(2,1)} %bitcast.8), custom_call_target="tpu_custom_call" | custom-call | tf_op jit(solution)/shard_map/project/pallas_call | solution.py:60
  3.2 0.5 %collective-permute-start = (f32[128,128]{1,0:T(8,128)S(1)}, f32[128,128]{1,0:T(8,128)S(1)}, u32[]{:S(2)}, u32[]{:S(2)}) collective-permute-start(f32[128,128]{1,0:T(8,128)S(1)} %project.1.mine), channel_id=1, source_target_pairs={{0,2},{2,0},{1,3},{3,1},{4,6},{6,4},{5,7},{7,5},{8,10},{10,8},{9,1... | collective-permute-start | bytes 196616 | tf_op jit(solution)/shard_map/ppermute | solution.py:274
  3.7 0.0 copy-done.1
  3.7 0.0 copy-done.2
  3.7 0.1 tags.1.marks
  3.8 0.8 %collective-permute-done.other = f32[128,128]{1,0:T(8,128)S(1)} collective-permute-done((f32[128,128]{1,0:T(8,128)S(1)}, f32[128,128]{1,0:T(8,128)S(1)}, u32[]{:S(2)}, u32[]{:S(2)}) %collective-permute-start) | collective-permute-done | bytes 65568 | tf_op jit(solution)/shard_map/ppermute | solution.py:274
  4.7 4.8 %collective-permute-start.1 = (f16[136,128]{1,0:T(8,128)(2,1)S(1)}, f16[136,128]{1,0:T(8,128)(2,1)S(1)}, u32[]{:S(2)}, u32[]{:S(2)}) collective-permute-start(f16[136,128]{1,0:T(8,128)(2,1)S(1)} %get-tuple-element.6), channel_id=1, source_target_pairs={{0,14},{2,8},{4,10},{6,12},{8,6},{10,0},{12,2},{14,4},{1,15},{3,9}... | collective-permute-start | bytes 104456 | tf_op jit(solution)/shard_map/ppermute | solution.py:277
  9.5 0.5 %collective-permute-start.2 = (f16[136,128]{1,0:T(8,128)(2,1)S(1)}, f16[136,128]{1,0:T(8,128)(2,1)S(1)}, u32[]{:S(2)}, u32[]{:S(2)}) collective-permute-start(f16[136,128]{1,0:T(8,128)(2,1)S(1)} %get-tuple-element.6), channel_id=1, source_target_pairs={{0,6},{2,4},{4,2},{6,0},{8,14},{10,12},{12,10},{14,8},{1,7},{3,5},... | collective-permute-start | bytes 104456 | tf_op jit(solution)/shard_map/ppermute | solution.py:277
  10.0 0.0 copy-done
  10.0 0.3 %turn.1.train = bf16[4096,128]{1,0:T(8,128)(2,1)S(1)} custom-call(bf16[128,4096]{1,0:T(8,128)(2,1)S(1)} %bitcast.5), custom_call_target="tpu_custom_call" | custom-call | tf_op jit(solution)/shard_map/turn/pallas_call | solution.py:126
  10.3 0.6 %own.1.scored = f32[32,128]{1,0:T(8,128)S(1)} custom-call(f32[136,128]{1,0:T(8,128)S(1)} %get-tuple-element.5.own, bf16[4096,128]{1,0:T(8,128)(2,1)S(1)} %turn.1.train), custom_call_target="tpu_custom_call" | custom-call | tf_op jit(solution)/shard_map/own/pallas_call | solution.py:260
  11.0 0.1 collective-permute-done.1
  11.1 0.6 %far.1.first = f32[32,128]{1,0:T(8,128)S(1)} custom-call(f32[32,128]{1,0:T(8,128)S(1)} %own.1.scored, f32[136,128]{1,0:T(8,128)S(1)} %convert_element_type.20.far, bf16[4096,128]{1,0:T(8,128)(2,1)S(1)} %turn.1.train), custom_call_target="tpu_custom_call" | custom-call | tf_op jit(solution)/shard_map/far/pallas_call | solution.py:260
  11.7 1.1 %collective-permute-done.2 = f16[136,128]{1,0:T(8,128)(2,1)S(1)} collective-permute-done((f16[136,128]{1,0:T(8,128)(2,1)S(1)}, f16[136,128]{1,0:T(8,128)(2,1)S(1)}, u32[]{:S(2)}, u32[]{:S(2)}) %collective-permute-start.2) | collective-permute-done | bytes 34848 | tf_op jit(solution)/shard_map/ppermute | solution.py:277
  12.9 1.1 %collective-permute-start.3 = (bf16[32,128]{1,0:T(8,128)(2,1)S(1)}, bf16[32,128]{1,0:T(8,128)(2,1)S(1)}, u32[]{:S(2)}, u32[]{:S(2)}) collective-permute-start(bf16[32,128]{1,0:T(8,128)(2,1)S(1)} %convert_element_type.22), channel_id=1, source_target_pairs={{0,3},{2,1},{1,2},{3,0},{4,7},{6,5},{5,6},{7,4},{8,11},{10,9},{9,1... | collective-permute-start | bytes 24584 | tf_op jit(solution)/shard_map/ppermute | solution.py:284
  14.0 2.1 %collective-permute-done.3 = bf16[32,128]{1,0:T(8,128)(2,1)S(1)} collective-permute-done((bf16[32,128]{1,0:T(8,128)(2,1)S(1)}, bf16[32,128]{1,0:T(8,128)(2,1)S(1)}, u32[]{:S(2)}, u32[]{:S(2)}) %collective-permute-start.3) | collective-permute-done | bytes 8224 | tf_op jit(solution)/shard_map/ppermute | solution.py:284
  16.1 0.2 %collective-permute-start.4 = (f32[64,128]{1,0:T(8,128)S(1)}, f32[64,128]{1,0:T(8,128)S(1)}, u32[]{:S(2)}, u32[]{:S(2)}) collective-permute-start(f32[64,128]{1,0:T(8,128)S(1)} %maximum_select_fusion), channel_id=1, source_target_pairs={{0,2},{2,0},{1,3},{3,1},{4,6},{6,4},{5,7},{7,5},{8,10},{10,8},{9,1... | collective-permute-start | bytes 98312 | tf_op jit(solution)/shard_map/ppermute | solution.py:274
  16.2 1.1 %collective-permute-done.4 = f32[64,128]{1,0:T(8,128)S(1)} collective-permute-done((f32[64,128]{1,0:T(8,128)S(1)}, f32[64,128]{1,0:T(8,128)S(1)}, u32[]{:S(2)}, u32[]{:S(2)}) %collective-permute-start.4) | collective-permute-done | bytes 32800 | tf_op jit(solution)/shard_map/ppermute | solution.py:274
  17.3 0.6 %add.12 = f32[64,128]{1,0:T(8,128)} add(f32[64,128]{1,0:T(8,128)S(1)} %maximum_select_fusion, f32[64,128]{1,0:T(8,128)S(1)} %collective-permute-done.4) | non-fusion elementwise | flops 8192 | bytes 98304 | tf_op jit(solution)/shard_map/add | solution.py:299
  (9 shorter events, 0.1 us)
Async XLA Ops:
  0.0 3.7 %copy-start.1 = (s32[1,32]{1,0:T(1,128)S(1)}, s32[1,32]{1,0:T(1,128)}, u32[]{:S(2)}) copy-start(s32[1,32]{1,0:T(1,128)} %lengths.1) | copy-start | bytes 388
  0.0 3.7 %copy-start.2 = (s32[1,32]{1,0:T(1,128)S(1)}, s32[1,32]{1,0:T(1,128)}, u32[]{:S(2)}) copy-start(s32[1,32]{1,0:T(1,128)} %query_ids.1) | copy-start | bytes 388
  0.0 10.0 %copy-start = (bf16[1,128,4096]{2,1,0:T(8,128)(2,1)S(1)}, bf16[1,128,4096]{2,1,0:T(8,128)(2,1)}, u32[]{:S(2)}) copy-start(bf16[1,128,4096]{2,1,0:T(8,128)(2,1)} %param.13) | copy-start | bytes 3145732
  3.2 1.4 %collective-permute-start = (f32[128,128]{1,0:T(8,128)S(1)}, f32[128,128]{1,0:T(8,128)S(1)}, u32[]{:S(2)}, u32[]{:S(2)}) collective-permute-start(f32[128,128]{1,0:T(8,128)S(1)} %project.1.mine), channel_id=1, source_target_pairs={{0,2},{2,0},{1,3},{3,1},{4,6},{6,4},{5,7},{7,5},{8,10},{10,8},{9,1... | collective-permute-start | bytes 196616 | tf_op jit(solution)/shard_map/ppermute | solution.py:274
  4.7 6.4 %collective-permute-start.1 = (f16[136,128]{1,0:T(8,128)(2,1)S(1)}, f16[136,128]{1,0:T(8,128)(2,1)S(1)}, u32[]{:S(2)}, u32[]{:S(2)}) collective-permute-start(f16[136,128]{1,0:T(8,128)(2,1)S(1)} %get-tuple-element.6), channel_id=1, source_target_pairs={{0,14},{2,8},{4,10},{6,12},{8,6},{10,0},{12,2},{14,4},{1,15},{3,9}... | collective-permute-start | bytes 104456 | tf_op jit(solution)/shard_map/ppermute | solution.py:277
  9.5 3.4 %collective-permute-start.2 = (f16[136,128]{1,0:T(8,128)(2,1)S(1)}, f16[136,128]{1,0:T(8,128)(2,1)S(1)}, u32[]{:S(2)}, u32[]{:S(2)}) collective-permute-start(f16[136,128]{1,0:T(8,128)(2,1)S(1)} %get-tuple-element.6), channel_id=1, source_target_pairs={{0,6},{2,4},{4,2},{6,0},{8,14},{10,12},{12,10},{14,8},{1,7},{3,5},... | collective-permute-start | bytes 104456 | tf_op jit(solution)/shard_map/ppermute | solution.py:277
  12.9 3.2 %collective-permute-start.3 = (bf16[32,128]{1,0:T(8,128)(2,1)S(1)}, bf16[32,128]{1,0:T(8,128)(2,1)S(1)}, u32[]{:S(2)}, u32[]{:S(2)}) collective-permute-start(bf16[32,128]{1,0:T(8,128)(2,1)S(1)} %convert_element_type.22), channel_id=1, source_target_pairs={{0,3},{2,1},{1,2},{3,0},{4,7},{6,5},{5,6},{7,4},{8,11},{10,9},{9,1... | collective-permute-start | bytes 24584 | tf_op jit(solution)/shard_map/ppermute | solution.py:284
  16.1 1.3 %collective-permute-start.4 = (f32[64,128]{1,0:T(8,128)S(1)}, f32[64,128]{1,0:T(8,128)S(1)}, u32[]{:S(2)}, u32[]{:S(2)}) collective-permute-start(f32[64,128]{1,0:T(8,128)S(1)} %maximum_select_fusion), channel_id=1, source_target_pairs={{0,2},{2,0},{1,3},{3,1},{4,6},{6,4},{5,7},{7,5},{8,10},{10,8},{9,1... | collective-permute-start | bytes 98312 | tf_op jit(solution)/shard_map/ppermute | solution.py:274

commit v4 on v3

--- a/solution.py
+++ b/solution.py
@@ -288,7 +288,9 @@
         )
 
     def four_by_two(own, train, queries):
-        far, near = (hand(own, steps).astype(jnp.float32) for steps in ((2, 3), (1, 1)))
+        far = hand(own, (2, 3)).astype(jnp.float32)
+        pairs = [pair for d in range(n_dp) for pair in ((d * cores, (d ^ 1) * cores + 1), (d * cores + 1, d * cores))]
+        near = lax.ppermute(own, ("dp", "tensor"), pairs).astype(jnp.float32)
         scored = _score_call(functools.partial(_own_kernel, queries), queries, "own", own.astype(jnp.float32), train)
         first = _score_call(functools.partial(_far_kernel, queries), queries, "far", scored, far, train)
         sent = _score_call(functools.partial(_sent_kernel, queries), queries, "sent", first, near, train)

time: 18.1 us -> 17.4 us (0.961)
  waiting for transfers between devices: 5.16 us -> 3.4 us
  starting transfers between devices: 7.12 us -> 8.15 us
    ppermute x2 -> x1, waiting for transfers between devices: 1.21 us -> 0.11 us  [hand(): lax.ppermute(v, ('dp', 'tensor'), [(d * cores + t, (d ^ steps[1 - t]) * c...]
    ppermute x1, starting transfers between devices: 1.13 us -> 2.19 us  [hand_section(): lax.ppermute(v, ('tensor', 'section'), [(t * sections + s, (1 - t) * sect...]
    ppermute x1, waiting for transfers between devices: 2.05 us -> 1.36 us  [hand_section(): lax.ppermute(v, ('tensor', 'section'), [(t * sections + s, (1 - t) * sect...]
    ppermute x0 -> x1, starting transfers between devices: none -> 0.52 us  [four_by_two(): near = lax.ppermute(own, ('dp', 'tensor'), pairs).astype(jnp.float32)]
    ppermute x2 -> x1, starting transfers between devices: 5.29 us -> 4.77 us  [hand(): lax.ppermute(v, ('dp', 'tensor'), [(d * cores + t, (d ^ steps[1 - t]) * c...]
  transfers between devices with their start and end apart: 5 -> 5, of which waited for: 5 -> 4; matrix products, arithmetic and copies ran while one was open for 0% -> 0% of each run, Pallas kernels for 9% -> 10%
where the time goes in v4:
time: 17.4 us; the launch traced here: 17.3 us
  starting transfers between devices  8.15 us (47%)
  Pallas kernels  4.94 us (28%)
  waiting for transfers between devices  3.4 us (20%)
  other arithmetic  0.66 us (4%)
    ppermute x1, starting transfers between devices, hand(): lax.ppermute(v, ('dp', 'tensor'), [(d * cores + t, (d ^ steps[1 - t]) * c...  4.77 us
    pallas_call x1, Pallas kernels, project(): pl.pallas_call(_project_kernel, out_shape=jax.ShapeDtypeStruct((2 * RANK,...  3.19 us
    ppermute x1, starting transfers between devices, hand_section(): lax.ppermute(v, ('tensor', 'section'), [(t * sections + s, (1 - t) * sect...  2.19 us
    ppermute x2, waiting for transfers between devices, swap(): return lax.ppermute(v, 'tensor', [(0, 1), (1, 0)])  1.92 us
    ppermute x1, waiting for transfers between devices, hand_section(): lax.ppermute(v, ('tensor', 'section'), [(t * sections + s, (1 - t) * sect...  1.36 us
    pallas_call x4, Pallas kernels, _score_call(): pl.pallas_call(kernel, out_shape=jax.ShapeDtypeStruct((queries, args[-1]....  1.31 us
    ppermute x2, starting transfers between devices, swap(): return lax.ppermute(v, 'tensor', [(0, 1), (1, 0)])  0.67 us
    add x1, other arithmetic, four_by_two(): return both + swap(both)  0.62 us
  transfers between devices with their start and end apart: 5, of which 4 were waited for; matrix products, arithmetic and copies ran while one was open for 0% of the time, Pallas kernels for 10%

profile of v4, /device:TPU:0, one launch (start us, length us, event | category | flops | bytes accessed | tf_op | source)
XLA Modules:
  0.0 17.3 jit_solution(864317900657761286)
XLA Ops:
  0.0 0.0 copy-start.1
  0.0 0.0 copy-start.2
  0.0 0.0 copy-start
  0.0 3.2 %project.1.mine = f32[128,128]{1,0:T(8,128)S(1)} custom-call(bf16[128,4096]{1,0:T(8,128)(2,1)} %bitcast.7, bf16[128,7168]{1,0:T(8,128)(2,1)} %bitcast.6, bf16[64,4096]{1,0:T(8,128)(2,1)} %bitcast.9, bf16[64,7168]{1,0:T(8,128)(2,1)} %bitcast.8), custom_call_target="tpu_custom_call" | custom-call | tf_op jit(solution)/shard_map/project/pallas_call | solution.py:60
  3.2 0.5 %collective-permute-start = (f32[128,128]{1,0:T(8,128)S(1)}, f32[128,128]{1,0:T(8,128)S(1)}, u32[]{:S(2)}, u32[]{:S(2)}) collective-permute-start(f32[128,128]{1,0:T(8,128)S(1)} %project.1.mine), channel_id=1, source_target_pairs={{0,2},{2,0},{1,3},{3,1},{4,6},{6,4},{5,7},{7,5},{8,10},{10,8},{9,1... | collective-permute-start | bytes 196616 | tf_op jit(solution)/shard_map/ppermute | solution.py:274
  3.7 0.0 copy-done.1
  3.7 0.0 copy-done.2
  3.7 0.1 tags.1.marks
  3.8 0.8 %collective-permute-done.other = f32[128,128]{1,0:T(8,128)S(1)} collective-permute-done((f32[128,128]{1,0:T(8,128)S(1)}, f32[128,128]{1,0:T(8,128)S(1)}, u32[]{:S(2)}, u32[]{:S(2)}) %collective-permute-start) | collective-permute-done | bytes 65568 | tf_op jit(solution)/shard_map/ppermute | solution.py:274
  4.7 4.8 %collective-permute-start.1 = (f16[136,128]{1,0:T(8,128)(2,1)S(1)}, f16[136,128]{1,0:T(8,128)(2,1)S(1)}, u32[]{:S(2)}, u32[]{:S(2)}) collective-permute-start(f16[136,128]{1,0:T(8,128)(2,1)S(1)} %get-tuple-element.6), channel_id=1, source_target_pairs={{0,14},{2,8},{4,10},{6,12},{8,6},{10,0},{12,2},{14,4},{1,15},{3,9}... | collective-permute-start | bytes 104456 | tf_op jit(solution)/shard_map/ppermute | solution.py:277
  9.5 0.5 %collective-permute-start.2 = (f16[136,128]{1,0:T(8,128)(2,1)S(1)}, f16[136,128]{1,0:T(8,128)(2,1)S(1)}, u32[]{:S(2)}, u32[]{:S(2)}) collective-permute-start(f16[136,128]{1,0:T(8,128)(2,1)S(1)} %get-tuple-element.6), channel_id=1, source_target_pairs={{0,6},{2,0},{4,2},{6,4},{8,14},{10,8},{12,10},{14,12},{1,7},{3,1},... | collective-permute-start | bytes 104456 | tf_op jit(solution)/shard_map/ppermute | solution.py:293
  10.0 0.0 copy-done
  10.0 0.3 %turn.1.train = bf16[4096,128]{1,0:T(8,128)(2,1)S(1)} custom-call(bf16[128,4096]{1,0:T(8,128)(2,1)S(1)} %bitcast.5), custom_call_target="tpu_custom_call" | custom-call | tf_op jit(solution)/shard_map/turn/pallas_call | solution.py:126
  10.3 0.6 %own.1.scored = f32[32,128]{1,0:T(8,128)S(1)} custom-call(f32[136,128]{1,0:T(8,128)S(1)} %get-tuple-element.5.own, bf16[4096,128]{1,0:T(8,128)(2,1)S(1)} %turn.1.train), custom_call_target="tpu_custom_call" | custom-call | tf_op jit(solution)/shard_map/own/pallas_call | solution.py:260
  11.0 0.1 collective-permute-done.1
  11.1 0.6 %far.1.first = f32[32,128]{1,0:T(8,128)S(1)} custom-call(f32[32,128]{1,0:T(8,128)S(1)} %own.1.scored, f32[136,128]{1,0:T(8,128)S(1)} %convert_element_type.20.far, bf16[4096,128]{1,0:T(8,128)(2,1)S(1)} %turn.1.train), custom_call_target="tpu_custom_call" | custom-call | tf_op jit(solution)/shard_map/far/pallas_call | solution.py:260
  11.7 0.0 collective-permute-done.2
  11.8 2.2 %collective-permute-start.3 = (bf16[32,128]{1,0:T(8,128)(2,1)S(1)}, bf16[32,128]{1,0:T(8,128)(2,1)S(1)}, u32[]{:S(2)}, u32[]{:S(2)}) collective-permute-start(bf16[32,128]{1,0:T(8,128)(2,1)S(1)} %convert_element_type.22), channel_id=1, source_target_pairs={{0,3},{2,1},{1,2},{3,0},{4,7},{6,5},{5,6},{7,4},{8,11},{10,9},{9,1... | collective-permute-start | bytes 24584 | tf_op jit(solution)/shard_map/ppermute | solution.py:284
  14.0 1.4 %collective-permute-done.3 = bf16[32,128]{1,0:T(8,128)(2,1)S(1)} collective-permute-done((bf16[32,128]{1,0:T(8,128)(2,1)S(1)}, bf16[32,128]{1,0:T(8,128)(2,1)S(1)}, u32[]{:S(2)}, u32[]{:S(2)}) %collective-permute-start.3) | collective-permute-done | bytes 8224 | tf_op jit(solution)/shard_map/ppermute | solution.py:284
  15.4 0.2 collective-permute-start.4
  15.5 1.1 %collective-permute-done.4 = f32[64,128]{1,0:T(8,128)S(1)} collective-permute-done((f32[64,128]{1,0:T(8,128)S(1)}, f32[64,128]{1,0:T(8,128)S(1)}, u32[]{:S(2)}, u32[]{:S(2)}) %collective-permute-start.4) | collective-permute-done | bytes 32800 | tf_op jit(solution)/shard_map/ppermute | solution.py:274
  16.6 0.6 %add.12 = f32[64,128]{1,0:T(8,128)} add(f32[64,128]{1,0:T(8,128)S(1)} %maximum_select_fusion, f32[64,128]{1,0:T(8,128)S(1)} %collective-permute-done.4) | non-fusion elementwise | flops 8192 | bytes 98304 | tf_op jit(solution)/shard_map/add | solution.py:301
  (9 shorter events, 0.1 us)
Async XLA Ops:
  0.0 3.7 %copy-start.1 = (s32[1,32]{1,0:T(1,128)S(1)}, s32[1,32]{1,0:T(1,128)}, u32[]{:S(2)}) copy-start(s32[1,32]{1,0:T(1,128)} %lengths.1) | copy-start | bytes 388
  0.0 3.7 %copy-start.2 = (s32[1,32]{1,0:T(1,128)S(1)}, s32[1,32]{1,0:T(1,128)}, u32[]{:S(2)}) copy-start(s32[1,32]{1,0:T(1,128)} %query_ids.1) | copy-start | bytes 388
  0.0 10.0 %copy-start = (bf16[1,128,4096]{2,1,0:T(8,128)(2,1)S(1)}, bf16[1,128,4096]{2,1,0:T(8,128)(2,1)}, u32[]{:S(2)}) copy-start(bf16[1,128,4096]{2,1,0:T(8,128)(2,1)} %param.13) | copy-start | bytes 3145732
  3.2 1.4 %collective-permute-start = (f32[128,128]{1,0:T(8,128)S(1)}, f32[128,128]{1,0:T(8,128)S(1)}, u32[]{:S(2)}, u32[]{:S(2)}) collective-permute-start(f32[128,128]{1,0:T(8,128)S(1)} %project.1.mine), channel_id=1, source_target_pairs={{0,2},{2,0},{1,3},{3,1},{4,6},{6,4},{5,7},{7,5},{8,10},{10,8},{9,1... | collective-permute-start | bytes 196616 | tf_op jit(solution)/shard_map/ppermute | solution.py:274
  4.7 6.4 %collective-permute-start.1 = (f16[136,128]{1,0:T(8,128)(2,1)S(1)}, f16[136,128]{1,0:T(8,128)(2,1)S(1)}, u32[]{:S(2)}, u32[]{:S(2)}) collective-permute-start(f16[136,128]{1,0:T(8,128)(2,1)S(1)} %get-tuple-element.6), channel_id=1, source_target_pairs={{0,14},{2,8},{4,10},{6,12},{8,6},{10,0},{12,2},{14,4},{1,15},{3,9}... | collective-permute-start | bytes 104456 | tf_op jit(solution)/shard_map/ppermute | solution.py:277
  9.5 2.3 %collective-permute-start.2 = (f16[136,128]{1,0:T(8,128)(2,1)S(1)}, f16[136,128]{1,0:T(8,128)(2,1)S(1)}, u32[]{:S(2)}, u32[]{:S(2)}) collective-permute-start(f16[136,128]{1,0:T(8,128)(2,1)S(1)} %get-tuple-element.6), channel_id=1, source_target_pairs={{0,6},{2,0},{4,2},{6,4},{8,14},{10,8},{12,10},{14,12},{1,7},{3,1},... | collective-permute-start | bytes 104456 | tf_op jit(solution)/shard_map/ppermute | solution.py:293
  11.8 3.6 %collective-permute-start.3 = (bf16[32,128]{1,0:T(8,128)(2,1)S(1)}, bf16[32,128]{1,0:T(8,128)(2,1)S(1)}, u32[]{:S(2)}, u32[]{:S(2)}) collective-permute-start(bf16[32,128]{1,0:T(8,128)(2,1)S(1)} %convert_element_type.22), channel_id=1, source_target_pairs={{0,3},{2,1},{1,2},{3,0},{4,7},{6,5},{5,6},{7,4},{8,11},{10,9},{9,1... | collective-permute-start | bytes 24584 | tf_op jit(solution)/shard_map/ppermute | solution.py:284
  15.4 1.3 %collective-permute-start.4 = (f32[64,128]{1,0:T(8,128)S(1)}, f32[64,128]{1,0:T(8,128)S(1)}, u32[]{:S(2)}, u32[]{:S(2)}) collective-permute-start(f32[64,128]{1,0:T(8,128)S(1)} %maximum_select_fusion), channel_id=1, source_target_pairs={{0,2},{2,0},{1,3},{3,1},{4,6},{6,4},{5,7},{7,5},{8,10},{10,8},{9,1... | collective-permute-start | bytes 98312 | tf_op jit(solution)/shard_map/ppermute | solution.py:274

commit v5 on v4

--- a/solution.py
+++ b/solution.py
@@ -294,7 +294,7 @@
         scored = _score_call(functools.partial(_own_kernel, queries), queries, "own", own.astype(jnp.float32), train)
         first = _score_call(functools.partial(_far_kernel, queries), queries, "far", scored, far, train)
         sent = _score_call(functools.partial(_sent_kernel, queries), queries, "sent", first, near, train)
-        got = hand_section(sent.astype(jnp.bfloat16), 1).astype(jnp.float32)
+        got = hand_section(sent, 1)
         kept = _score_call(functools.partial(_kept_kernel, queries), queries, "kept", scored, far, near, train)
         kept_first = (lax.axis_index("dp") + lax.axis_index("tensor")) % 2 == 0
         both = jnp.where(kept_first, jnp.concatenate([kept, got]), jnp.concatenate([got, kept]))

time: 17.4 us -> 17.4 us (level)
  no operation moved by 1% of the time
where the time goes in v5:
time: 17.4 us; the launch traced here: 17.2 us
  starting transfers between devices  8.1 us (47%)
  Pallas kernels  4.94 us (28%)
  waiting for transfers between devices  3.47 us (20%)
  other arithmetic  0.65 us (4%)
    ppermute x1, starting transfers between devices, hand(): lax.ppermute(v, ('dp', 'tensor'), [(d * cores + t, (d ^ steps[1 - t]) * c...  4.77 us
    pallas_call x1, Pallas kernels, project(): pl.pallas_call(_project_kernel, out_shape=jax.ShapeDtypeStruct((2 * RANK,...  3.19 us
    ppermute x1, starting transfers between devices, hand_section(): lax.ppermute(v, ('tensor', 'section'), [(t * sections + s, (1 - t) * sect...  2.19 us
    ppermute x2, waiting for transfers between devices, swap(): return lax.ppermute(v, 'tensor', [(0, 1), (1, 0)])  1.91 us
    ppermute x1, waiting for transfers between devices, hand_section(): lax.ppermute(v, ('tensor', 'section'), [(t * sections + s, (1 - t) * sect...  1.44 us
    pallas_call x4, Pallas kernels, _score_call(): pl.pallas_call(kernel, out_shape=jax.ShapeDtypeStruct((queries, args[-1]....  1.31 us
    add x1, other arithmetic, four_by_two(): return both + swap(both)  0.62 us
    ppermute x2, starting transfers between devices, swap(): return lax.ppermute(v, 'tensor', [(0, 1), (1, 0)])  0.61 us
  transfers between devices with their start and end apart: 5, of which 4 were waited for; matrix products, arithmetic and copies ran while one was open for 0% of the time, Pallas kernels for 10%

profile of v5, /device:TPU:0, one launch (start us, length us, event | category | flops | bytes accessed | tf_op | source)
XLA Modules:
  0.0 17.2 jit_solution(10074623099696739890)
XLA Ops:
  0.0 0.0 copy-start.1
  0.0 0.0 copy-start.2
  0.0 0.0 copy-start
  0.0 3.2 %project.1.mine = f32[128,128]{1,0:T(8,128)S(1)} custom-call(bf16[128,4096]{1,0:T(8,128)(2,1)} %bitcast.7, bf16[128,7168]{1,0:T(8,128)(2,1)} %bitcast.6, bf16[64,4096]{1,0:T(8,128)(2,1)} %bitcast.9, bf16[64,7168]{1,0:T(8,128)(2,1)} %bitcast.8), custom_call_target="tpu_custom_call" | custom-call | tf_op jit(solution)/shard_map/project/pallas_call | solution.py:60
  3.2 0.5 %collective-permute-start = (f32[128,128]{1,0:T(8,128)S(1)}, f32[128,128]{1,0:T(8,128)S(1)}, u32[]{:S(2)}, u32[]{:S(2)}) collective-permute-start(f32[128,128]{1,0:T(8,128)S(1)} %project.1.mine), channel_id=1, source_target_pairs={{0,2},{2,0},{1,3},{3,1},{4,6},{6,4},{5,7},{7,5},{8,10},{10,8},{9,1... | collective-permute-start | bytes 196616 | tf_op jit(solution)/shard_map/ppermute | solution.py:274
  3.7 0.0 copy-done.1
  3.7 0.0 copy-done.2
  3.7 0.1 tags.1.marks
  3.8 0.8 %collective-permute-done.other = f32[128,128]{1,0:T(8,128)S(1)} collective-permute-done((f32[128,128]{1,0:T(8,128)S(1)}, f32[128,128]{1,0:T(8,128)S(1)}, u32[]{:S(2)}, u32[]{:S(2)}) %collective-permute-start) | collective-permute-done | bytes 65568 | tf_op jit(solution)/shard_map/ppermute | solution.py:274
  4.7 4.8 %collective-permute-start.1 = (f16[136,128]{1,0:T(8,128)(2,1)S(1)}, f16[136,128]{1,0:T(8,128)(2,1)S(1)}, u32[]{:S(2)}, u32[]{:S(2)}) collective-permute-start(f16[136,128]{1,0:T(8,128)(2,1)S(1)} %get-tuple-element.6), channel_id=1, source_target_pairs={{0,14},{2,8},{4,10},{6,12},{8,6},{10,0},{12,2},{14,4},{1,15},{3,9}... | collective-permute-start | bytes 104456 | tf_op jit(solution)/shard_map/ppermute | solution.py:277
  9.5 0.5 %collective-permute-start.2 = (f16[136,128]{1,0:T(8,128)(2,1)S(1)}, f16[136,128]{1,0:T(8,128)(2,1)S(1)}, u32[]{:S(2)}, u32[]{:S(2)}) collective-permute-start(f16[136,128]{1,0:T(8,128)(2,1)S(1)} %get-tuple-element.6), channel_id=1, source_target_pairs={{0,6},{2,0},{4,2},{6,4},{8,14},{10,8},{12,10},{14,12},{1,7},{3,1},... | collective-permute-start | bytes 104456 | tf_op jit(solution)/shard_map/ppermute | solution.py:293
  10.0 0.0 copy-done
  10.0 0.3 %turn.1.train = bf16[4096,128]{1,0:T(8,128)(2,1)S(1)} custom-call(bf16[128,4096]{1,0:T(8,128)(2,1)S(1)} %bitcast.5), custom_call_target="tpu_custom_call" | custom-call | tf_op jit(solution)/shard_map/turn/pallas_call | solution.py:126
  10.3 0.6 %own.1.scored = f32[32,128]{1,0:T(8,128)S(1)} custom-call(f32[136,128]{1,0:T(8,128)S(1)} %get-tuple-element.5.own, bf16[4096,128]{1,0:T(8,128)(2,1)S(1)} %turn.1.train), custom_call_target="tpu_custom_call" | custom-call | tf_op jit(solution)/shard_map/own/pallas_call | solution.py:260
  11.0 0.1 collective-permute-done.1
  11.1 0.6 %far.1.first = f32[32,128]{1,0:T(8,128)S(1)} custom-call(f32[32,128]{1,0:T(8,128)S(1)} %own.1.scored, f32[136,128]{1,0:T(8,128)S(1)} %convert_element_type.14.far, bf16[4096,128]{1,0:T(8,128)(2,1)S(1)} %turn.1.train), custom_call_target="tpu_custom_call" | custom-call | tf_op jit(solution)/shard_map/far/pallas_call | solution.py:260
  11.7 0.0 collective-permute-done.2
  11.8 2.2 %collective-permute-start.3 = (f32[32,128]{1,0:T(8,128)S(1)}, f32[32,128]{1,0:T(8,128)S(1)}, u32[]{:S(2)}, u32[]{:S(2)}) collective-permute-start(f32[32,128]{1,0:T(8,128)S(1)} %sent.1), channel_id=1, source_target_pairs={{0,3},{2,1},{1,2},{3,0},{4,7},{6,5},{5,6},{7,4},{8,11},{10,9},{9,1... | collective-permute-start | bytes 49160 | tf_op jit(solution)/shard_map/ppermute | solution.py:284
  14.0 1.4 %collective-permute-done.3 = f32[32,128]{1,0:T(8,128)S(1)} collective-permute-done((f32[32,128]{1,0:T(8,128)S(1)}, f32[32,128]{1,0:T(8,128)S(1)}, u32[]{:S(2)}, u32[]{:S(2)}) %collective-permute-start.3) | collective-permute-done | bytes 16416 | tf_op jit(solution)/shard_map/ppermute | solution.py:284
  15.4 0.1 collective-permute-start.4
  15.5 1.1 %collective-permute-done.4 = f32[64,128]{1,0:T(8,128)S(1)} collective-permute-done((f32[64,128]{1,0:T(8,128)S(1)}, f32[64,128]{1,0:T(8,128)S(1)}, u32[]{:S(2)}, u32[]{:S(2)}) %collective-permute-start.4) | collective-permute-done | bytes 32800 | tf_op jit(solution)/shard_map/ppermute | solution.py:274
  16.6 0.6 %add.12 = f32[64,128]{1,0:T(8,128)} add(f32[64,128]{1,0:T(8,128)S(1)} %maximum_select_fusion, f32[64,128]{1,0:T(8,128)S(1)} %collective-permute-done.4) | non-fusion elementwise | flops 8192 | bytes 98304 | tf_op jit(solution)/shard_map/add | solution.py:301
  (7 shorter events, 0.1 us)
Async XLA Ops:
  0.0 3.7 %copy-start.1 = (s32[1,32]{1,0:T(1,128)S(1)}, s32[1,32]{1,0:T(1,128)}, u32[]{:S(2)}) copy-start(s32[1,32]{1,0:T(1,128)} %lengths.1) | copy-start | bytes 388
  0.0 3.7 %copy-start.2 = (s32[1,32]{1,0:T(1,128)S(1)}, s32[1,32]{1,0:T(1,128)}, u32[]{:S(2)}) copy-start(s32[1,32]{1,0:T(1,128)} %query_ids.1) | copy-start | bytes 388
  0.0 10.0 %copy-start = (bf16[1,128,4096]{2,1,0:T(8,128)(2,1)S(1)}, bf16[1,128,4096]{2,1,0:T(8,128)(2,1)}, u32[]{:S(2)}) copy-start(bf16[1,128,4096]{2,1,0:T(8,128)(2,1)} %param.13) | copy-start | bytes 3145732
  3.2 1.4 %collective-permute-start = (f32[128,128]{1,0:T(8,128)S(1)}, f32[128,128]{1,0:T(8,128)S(1)}, u32[]{:S(2)}, u32[]{:S(2)}) collective-permute-start(f32[128,128]{1,0:T(8,128)S(1)} %project.1.mine), channel_id=1, source_target_pairs={{0,2},{2,0},{1,3},{3,1},{4,6},{6,4},{5,7},{7,5},{8,10},{10,8},{9,1... | collective-permute-start | bytes 196616 | tf_op jit(solution)/shard_map/ppermute | solution.py:274
  4.7 6.4 %collective-permute-start.1 = (f16[136,128]{1,0:T(8,128)(2,1)S(1)}, f16[136,128]{1,0:T(8,128)(2,1)S(1)}, u32[]{:S(2)}, u32[]{:S(2)}) collective-permute-start(f16[136,128]{1,0:T(8,128)(2,1)S(1)} %get-tuple-element.6), channel_id=1, source_target_pairs={{0,14},{2,8},{4,10},{6,12},{8,6},{10,0},{12,2},{14,4},{1,15},{3,9}... | collective-permute-start | bytes 104456 | tf_op jit(solution)/shard_map/ppermute | solution.py:277
  9.5 2.3 %collective-permute-start.2 = (f16[136,128]{1,0:T(8,128)(2,1)S(1)}, f16[136,128]{1,0:T(8,128)(2,1)S(1)}, u32[]{:S(2)}, u32[]{:S(2)}) collective-permute-start(f16[136,128]{1,0:T(8,128)(2,1)S(1)} %get-tuple-element.6), channel_id=1, source_target_pairs={{0,6},{2,0},{4,2},{6,4},{8,14},{10,8},{12,10},{14,12},{1,7},{3,1},... | collective-permute-start | bytes 104456 | tf_op jit(solution)/shard_map/ppermute | solution.py:293
  11.8 3.6 %collective-permute-start.3 = (f32[32,128]{1,0:T(8,128)S(1)}, f32[32,128]{1,0:T(8,128)S(1)}, u32[]{:S(2)}, u32[]{:S(2)}) collective-permute-start(f32[32,128]{1,0:T(8,128)S(1)} %sent.1), channel_id=1, source_target_pairs={{0,3},{2,1},{1,2},{3,0},{4,7},{6,5},{5,6},{7,4},{8,11},{10,9},{9,1... | collective-permute-start | bytes 49160 | tf_op jit(solution)/shard_map/ppermute | solution.py:284
  15.4 1.2 %collective-permute-start.4 = (f32[64,128]{1,0:T(8,128)S(1)}, f32[64,128]{1,0:T(8,128)S(1)}, u32[]{:S(2)}, u32[]{:S(2)}) collective-permute-start(f32[64,128]{1,0:T(8,128)S(1)} %maximum_select_fusion), channel_id=1, source_target_pairs={{0,2},{2,0},{1,3},{3,1},{4,6},{6,4},{5,7},{7,5},{8,10},{10,8},{9,1... | collective-permute-start | bytes 98312 | tf_op jit(solution)/shard_map/ppermute | solution.py:274

commit v6 on v5

--- a/solution.py
+++ b/solution.py
@@ -205,11 +205,11 @@
 
 
 def _own_kernel(queries, own, train, out):
-    @pl.when(lax.axis_index("tensor") == 0)
+    @pl.when(lax.axis_index("tensor") == 1)
     def _():
         out[...] = _unit(own, train, queries)
 
-    @pl.when(lax.axis_index("tensor") != 0)
+    @pl.when(lax.axis_index("tensor") != 1)
     def _():
         out[...] = jnp.zeros_like(out)
 
@@ -228,7 +228,7 @@
 
 def _sent_kernel(queries, first, near, train, out):
     sent = lax.axis_index("dp") // 2 == lax.axis_index("section")
-    use_near = jnp.logical_not(sent) & (lax.axis_index("tensor") != 0)
+    use_near = jnp.logical_not(sent) & (lax.axis_index("tensor") != 1)
 
     @pl.when(use_near)
     def _():
@@ -247,11 +247,11 @@
     def _():
         out[...] = _unit(far, train, queries)
 
-    @pl.when(sent & (core == 0))
+    @pl.when(sent & (core == 1))
     def _():
         out[...] = scored[...]
 
-    @pl.when(sent & (core != 0))
+    @pl.when(sent & (core != 1))
     def _():
         out[...] = _unit(near, train, queries)
 
@@ -288,15 +288,15 @@
         )
 
     def four_by_two(own, train, queries):
-        far = hand(own, (2, 3)).astype(jnp.float32)
-        pairs = [pair for d in range(n_dp) for pair in ((d * cores, (d ^ 1) * cores + 1), (d * cores + 1, d * cores))]
+        far = hand(own, (3, 2)).astype(jnp.float32)
+        pairs = [pair for d in range(n_dp) for pair in ((d * cores + 1, (d ^ 1) * cores), (d * cores, d * cores + 1))]
         near = lax.ppermute(own, ("dp", "tensor"), pairs).astype(jnp.float32)
         scored = _score_call(functools.partial(_own_kernel, queries), queries, "own", own.astype(jnp.float32), train)
         first = _score_call(functools.partial(_far_kernel, queries), queries, "far", scored, far, train)
         sent = _score_call(functools.partial(_sent_kernel, queries), queries, "sent", first, near, train)
         got = hand_section(sent, 1)
         kept = _score_call(functools.partial(_kept_kernel, queries), queries, "kept", scored, far, near, train)
-        kept_first = (lax.axis_index("dp") + lax.axis_index("tensor")) % 2 == 0
+        kept_first = (lax.axis_index("dp") + lax.axis_index("tensor")) % 2 == 1
         both = jnp.where(kept_first, jnp.concatenate([kept, got]), jnp.concatenate([got, kept]))
         return both + swap(both)
 

time: 17.4 us -> 17.2 us (0.989)
  starting transfers between devices: 8.1 us -> 6.58 us
  waiting for transfers between devices: 3.47 us -> 4.77 us
    ppermute x1, starting transfers between devices: 2.19 us -> 0.5 us  [hand_section(): lax.ppermute(v, ('tensor', 'section'), [(t * sections + s, (1 - t) * sect...]
    ppermute x1, starting transfers between devices: 4.77 us -> 3.76 us  [hand(): lax.ppermute(v, ('dp', 'tensor'), [(d * cores + t, (d ^ steps[1 - t]) * c...]
    ppermute x1, waiting for transfers between devices: 0.11 us -> 1.01 us  [hand(): lax.ppermute(v, ('dp', 'tensor'), [(d * cores + t, (d ^ steps[1 - t]) * c...]
    ppermute x1, starting transfers between devices: 0.52 us -> 1.37 us  [four_by_two(): near = lax.ppermute(own, ('dp', 'tensor'), pairs).astype(jnp.float32)]
    ppermute x1, waiting for transfers between devices: 1.44 us -> 2.1 us  [hand_section(): lax.ppermute(v, ('tensor', 'section'), [(t * sections + s, (1 - t) * sect...]
    ppermute x2, starting transfers between devices: 0.61 us -> 0.96 us  [swap(): return lax.ppermute(v, 'tensor', [(0, 1), (1, 0)])]
    ppermute x2, waiting for transfers between devices: 1.91 us -> 1.66 us  [swap(): return lax.ppermute(v, 'tensor', [(0, 1), (1, 0)])]
where the time goes in v6:
time: 17.2 us; the launch traced here: 17 us
  starting transfers between devices  6.58 us (38%)
  Pallas kernels  4.96 us (29%)
  waiting for transfers between devices  4.77 us (28%)
  other arithmetic  0.65 us (4%)
    ppermute x1, starting transfers between devices, hand(): lax.ppermute(v, ('dp', 'tensor'), [(d * cores + t, (d ^ steps[1 - t]) * c...  3.76 us
    pallas_call x1, Pallas kernels, project(): pl.pallas_call(_project_kernel, out_shape=jax.ShapeDtypeStruct((2 * RANK,...  3.19 us
    ppermute x1, waiting for transfers between devices, hand_section(): lax.ppermute(v, ('tensor', 'section'), [(t * sections + s, (1 - t) * sect...  2.1 us
    ppermute x2, waiting for transfers between devices, swap(): return lax.ppermute(v, 'tensor', [(0, 1), (1, 0)])  1.66 us
    ppermute x1, starting transfers between devices, four_by_two(): near = lax.ppermute(own, ('dp', 'tensor'), pairs).astype(jnp.float32)  1.37 us
    pallas_call x4, Pallas kernels, _score_call(): pl.pallas_call(kernel, out_shape=jax.ShapeDtypeStruct((queries, args[-1]....  1.32 us
    ppermute x1, waiting for transfers between devices, hand(): lax.ppermute(v, ('dp', 'tensor'), [(d * cores + t, (d ^ steps[1 - t]) * c...  1.01 us
    ppermute x2, starting transfers between devices, swap(): return lax.ppermute(v, 'tensor', [(0, 1), (1, 0)])  0.96 us
  transfers between devices with their start and end apart: 5, of which 4 were waited for; matrix products, arithmetic and copies ran while one was open for 0% of the time, Pallas kernels for 10%

profile of v6, /device:TPU:0, one launch (start us, length us, event | category | flops | bytes accessed | tf_op | source)
XLA Modules:
  0.0 17.0 jit_solution(10753845197345145363)
XLA Ops:
  0.0 0.0 copy-start.1
  0.0 0.0 copy-start.2
  0.0 0.0 copy-start
  0.0 3.2 %project.1.mine = f32[128,128]{1,0:T(8,128)S(1)} custom-call(bf16[128,4096]{1,0:T(8,128)(2,1)} %bitcast.7, bf16[128,7168]{1,0:T(8,128)(2,1)} %bitcast.6, bf16[64,4096]{1,0:T(8,128)(2,1)} %bitcast.9, bf16[64,7168]{1,0:T(8,128)(2,1)} %bitcast.8), custom_call_target="tpu_custom_call" | custom-call | tf_op jit(solution)/shard_map/project/pallas_call | solution.py:60
  3.2 0.5 %collective-permute-start = (f32[128,128]{1,0:T(8,128)S(1)}, f32[128,128]{1,0:T(8,128)S(1)}, u32[]{:S(2)}, u32[]{:S(2)}) collective-permute-start(f32[128,128]{1,0:T(8,128)S(1)} %project.1.mine), channel_id=1, source_target_pairs={{0,2},{2,0},{1,3},{3,1},{4,6},{6,4},{5,7},{7,5},{8,10},{10,8},{9,1... | collective-permute-start | bytes 196616 | tf_op jit(solution)/shard_map/ppermute | solution.py:274
  3.7 0.0 copy-done.1
  3.7 0.0 copy-done.2
  3.7 0.1 tags.1.marks
  3.8 0.8 %collective-permute-done.other = f32[128,128]{1,0:T(8,128)S(1)} collective-permute-done((f32[128,128]{1,0:T(8,128)S(1)}, f32[128,128]{1,0:T(8,128)S(1)}, u32[]{:S(2)}, u32[]{:S(2)}) %collective-permute-start) | collective-permute-done | bytes 65568 | tf_op jit(solution)/shard_map/ppermute | solution.py:274
  4.7 3.8 %collective-permute-start.1 = (f16[136,128]{1,0:T(8,128)(2,1)S(1)}, f16[136,128]{1,0:T(8,128)(2,1)S(1)}, u32[]{:S(2)}, u32[]{:S(2)}) collective-permute-start(f16[136,128]{1,0:T(8,128)(2,1)S(1)} %get-tuple-element.6), channel_id=1, source_target_pairs={{0,10},{2,12},{4,14},{6,8},{8,2},{10,4},{12,6},{14,0},{1,11},{3,13... | collective-permute-start | bytes 104456 | tf_op jit(solution)/shard_map/ppermute | solution.py:277
  8.4 1.4 %collective-permute-start.2 = (f16[136,128]{1,0:T(8,128)(2,1)S(1)}, f16[136,128]{1,0:T(8,128)(2,1)S(1)}, u32[]{:S(2)}, u32[]{:S(2)}) collective-permute-start(f16[136,128]{1,0:T(8,128)(2,1)S(1)} %get-tuple-element.6), channel_id=1, source_target_pairs={{2,4},{0,2},{6,0},{4,6},{10,12},{8,10},{14,8},{12,14},{3,5},{1,3},... | collective-permute-start | bytes 104456 | tf_op jit(solution)/shard_map/ppermute | solution.py:293
  9.8 0.0 copy-done
  9.8 0.3 %turn.1.train = bf16[4096,128]{1,0:T(8,128)(2,1)S(1)} custom-call(bf16[128,4096]{1,0:T(8,128)(2,1)S(1)} %bitcast.5), custom_call_target="tpu_custom_call" | custom-call | tf_op jit(solution)/shard_map/turn/pallas_call | solution.py:126
  10.2 1.0 %collective-permute-done.1 = f16[136,128]{1,0:T(8,128)(2,1)S(1)} collective-permute-done((f16[136,128]{1,0:T(8,128)(2,1)S(1)}, f16[136,128]{1,0:T(8,128)(2,1)S(1)}, u32[]{:S(2)}, u32[]{:S(2)}) %collective-permute-start.1) | collective-permute-done | bytes 34848 | tf_op jit(solution)/shard_map/ppermute | solution.py:277
  11.2 0.6 %far.1.first = f32[32,128]{1,0:T(8,128)S(1)} custom-call(f32[32,128]{1,0:T(8,128)S(1)} %own.1.scored, f32[136,128]{1,0:T(8,128)S(1)} %convert_element_type.14.far, bf16[4096,128]{1,0:T(8,128)(2,1)S(1)} %turn.1.train), custom_call_target="tpu_custom_call" | custom-call | tf_op jit(solution)/shard_map/far/pallas_call | solution.py:260
  11.8 0.0 collective-permute-done.2
  11.9 0.5 %collective-permute-start.3 = (f32[32,128]{1,0:T(8,128)S(1)}, f32[32,128]{1,0:T(8,128)S(1)}, u32[]{:S(2)}, u32[]{:S(2)}) collective-permute-start(f32[32,128]{1,0:T(8,128)S(1)} %sent.1), channel_id=1, source_target_pairs={{0,3},{2,1},{1,2},{3,0},{4,7},{6,5},{5,6},{7,4},{8,11},{10,9},{9,1... | collective-permute-start | bytes 49160 | tf_op jit(solution)/shard_map/ppermute | solution.py:284
  12.4 0.6 %kept.1 = f32[32,128]{1,0:T(8,128)S(1)} custom-call(f32[32,128]{1,0:T(8,128)S(1)} %own.1.scored, f32[136,128]{1,0:T(8,128)S(1)} %convert_element_type.14.far, f32[136,128]{1,0:T(8,128)S(1)} %convert_element_type.15.near, bf16[4096,128]{1,0:T(8,128)(2,1)S(1)} %turn.1.train), custom_call_target="tpu_custom_call" | custom-call | tf_op jit(solution)/shard_map/kept/pallas_call | solution.py:260
  13.0 2.1 %collective-permute-done.3 = f32[32,128]{1,0:T(8,128)S(1)} collective-permute-done((f32[32,128]{1,0:T(8,128)S(1)}, f32[32,128]{1,0:T(8,128)S(1)}, u32[]{:S(2)}, u32[]{:S(2)}) %collective-permute-start.3) | collective-permute-done | bytes 16416 | tf_op jit(solution)/shard_map/ppermute | solution.py:284
  15.1 0.4 %collective-permute-start.4 = (f32[64,128]{1,0:T(8,128)S(1)}, f32[64,128]{1,0:T(8,128)S(1)}, u32[]{:S(2)}, u32[]{:S(2)}) collective-permute-start(f32[64,128]{1,0:T(8,128)S(1)} %maximum_select_fusion), channel_id=1, source_target_pairs={{0,2},{2,0},{1,3},{3,1},{4,6},{6,4},{5,7},{7,5},{8,10},{10,8},{9,1... | collective-permute-start | bytes 98312 | tf_op jit(solution)/shard_map/ppermute | solution.py:274
  15.6 0.9 %collective-permute-done.4 = f32[64,128]{1,0:T(8,128)S(1)} collective-permute-done((f32[64,128]{1,0:T(8,128)S(1)}, f32[64,128]{1,0:T(8,128)S(1)}, u32[]{:S(2)}, u32[]{:S(2)}) %collective-permute-start.4) | collective-permute-done | bytes 32800 | tf_op jit(solution)/shard_map/ppermute | solution.py:274
  16.4 0.6 %add.12 = f32[64,128]{1,0:T(8,128)} add(f32[64,128]{1,0:T(8,128)S(1)} %maximum_select_fusion, f32[64,128]{1,0:T(8,128)S(1)} %collective-permute-done.4) | non-fusion elementwise | flops 8192 | bytes 98304 | tf_op jit(solution)/shard_map/add | solution.py:301
  (7 shorter events, 0.1 us)
Async XLA Ops:
  0.0 3.7 %copy-start.1 = (s32[1,32]{1,0:T(1,128)S(1)}, s32[1,32]{1,0:T(1,128)}, u32[]{:S(2)}) copy-start(s32[1,32]{1,0:T(1,128)} %lengths.1) | copy-start | bytes 388
  0.0 3.7 %copy-start.2 = (s32[1,32]{1,0:T(1,128)S(1)}, s32[1,32]{1,0:T(1,128)}, u32[]{:S(2)}) copy-start(s32[1,32]{1,0:T(1,128)} %query_ids.1) | copy-start | bytes 388
  0.0 9.8 %copy-start = (bf16[1,128,4096]{2,1,0:T(8,128)(2,1)S(1)}, bf16[1,128,4096]{2,1,0:T(8,128)(2,1)}, u32[]{:S(2)}) copy-start(bf16[1,128,4096]{2,1,0:T(8,128)(2,1)} %param.13) | copy-start | bytes 3145732
  3.2 1.4 %collective-permute-start = (f32[128,128]{1,0:T(8,128)S(1)}, f32[128,128]{1,0:T(8,128)S(1)}, u32[]{:S(2)}, u32[]{:S(2)}) collective-permute-start(f32[128,128]{1,0:T(8,128)S(1)} %project.1.mine), channel_id=1, source_target_pairs={{0,2},{2,0},{1,3},{3,1},{4,6},{6,4},{5,7},{7,5},{8,10},{10,8},{9,1... | collective-permute-start | bytes 196616 | tf_op jit(solution)/shard_map/ppermute | solution.py:274
  4.7 6.5 %collective-permute-start.1 = (f16[136,128]{1,0:T(8,128)(2,1)S(1)}, f16[136,128]{1,0:T(8,128)(2,1)S(1)}, u32[]{:S(2)}, u32[]{:S(2)}) collective-permute-start(f16[136,128]{1,0:T(8,128)(2,1)S(1)} %get-tuple-element.6), channel_id=1, source_target_pairs={{0,10},{2,12},{4,14},{6,8},{8,2},{10,4},{12,6},{14,0},{1,11},{3,13... | collective-permute-start | bytes 104456 | tf_op jit(solution)/shard_map/ppermute | solution.py:277
  8.4 3.4 %collective-permute-start.2 = (f16[136,128]{1,0:T(8,128)(2,1)S(1)}, f16[136,128]{1,0:T(8,128)(2,1)S(1)}, u32[]{:S(2)}, u32[]{:S(2)}) collective-permute-start(f16[136,128]{1,0:T(8,128)(2,1)S(1)} %get-tuple-element.6), channel_id=1, source_target_pairs={{2,4},{0,2},{6,0},{4,6},{10,12},{8,10},{14,8},{12,14},{3,5},{1,3},... | collective-permute-start | bytes 104456 | tf_op jit(solution)/shard_map/ppermute | solution.py:293
  11.9 3.2 %collective-permute-start.3 = (f32[32,128]{1,0:T(8,128)S(1)}, f32[32,128]{1,0:T(8,128)S(1)}, u32[]{:S(2)}, u32[]{:S(2)}) collective-permute-start(f32[32,128]{1,0:T(8,128)S(1)} %sent.1), channel_id=1, source_target_pairs={{0,3},{2,1},{1,2},{3,0},{4,7},{6,5},{5,6},{7,4},{8,11},{10,9},{9,1... | collective-permute-start | bytes 49160 | tf_op jit(solution)/shard_map/ppermute | solution.py:284
  15.1 1.3 %collective-permute-start.4 = (f32[64,128]{1,0:T(8,128)S(1)}, f32[64,128]{1,0:T(8,128)S(1)}, u32[]{:S(2)}, u32[]{:S(2)}) collective-permute-start(f32[64,128]{1,0:T(8,128)S(1)} %maximum_select_fusion), channel_id=1, source_target_pairs={{0,2},{2,0},{1,3},{3,1},{4,6},{6,4},{5,7},{7,5},{8,10},{10,8},{9,1... | collective-permute-start | bytes 98312 | tf_op jit(solution)/shard_map/ppermute | solution.py:274

commit v7 on v6

--- a/solution.py
+++ b/solution.py
@@ -28,7 +28,7 @@
 
 
 ACT_PARTS = (1,)
-GRAD_PARTS = (7, 5, 2)
+GRAD_PARTS = (7, 6, 1)
 
 
 def _project_kernel(acts, grads, pin, pout, out, av, gv, piv, pov, sem):

time: 17.2 us -> 17.2 us (level)
  no operation moved by 1% of the time
where the time goes in v7:
time: 17.2 us; the launch traced here: 17.1 us
  starting transfers between devices  6.59 us (38%)
  Pallas kernels  4.96 us (29%)
  waiting for transfers between devices  4.77 us (28%)
  other arithmetic  0.65 us (4%)
    ppermute x1, starting transfers between devices, hand(): lax.ppermute(v, ('dp', 'tensor'), [(d * cores + t, (d ^ steps[1 - t]) * c...  3.76 us
    pallas_call x1, Pallas kernels, project(): pl.pallas_call(_project_kernel, out_shape=jax.ShapeDtypeStruct((2 * RANK,...  3.19 us
    ppermute x1, waiting for transfers between devices, hand_section(): lax.ppermute(v, ('tensor', 'section'), [(t * sections + s, (1 - t) * sect...  2.09 us
    ppermute x2, waiting for transfers between devices, swap(): return lax.ppermute(v, 'tensor', [(0, 1), (1, 0)])  1.66 us
    ppermute x1, starting transfers between devices, four_by_two(): near = lax.ppermute(own, ('dp', 'tensor'), pairs).astype(jnp.float32)  1.36 us
    pallas_call x4, Pallas kernels, _score_call(): pl.pallas_call(kernel, out_shape=jax.ShapeDtypeStruct((queries, args[-1]....  1.32 us
    ppermute x1, waiting for transfers between devices, hand(): lax.ppermute(v, ('dp', 'tensor'), [(d * cores + t, (d ^ steps[1 - t]) * c...  1.01 us
    ppermute x2, starting transfers between devices, swap(): return lax.ppermute(v, 'tensor', [(0, 1), (1, 0)])  0.97 us
  transfers between devices with their start and end apart: 5, of which 4 were waited for; matrix products, arithmetic and copies ran while one was open for 0% of the time, Pallas kernels for 10%

profile of v7, /device:TPU:0, one launch (start us, length us, event | category | flops | bytes accessed | tf_op | source)
XLA Modules:
  0.0 17.1 jit_solution(8837897077677069595)
XLA Ops:
  0.0 0.0 copy-start.1
  0.0 0.0 copy-start.2
  0.0 0.0 copy-start
  0.0 3.2 %project.1.mine = f32[128,128]{1,0:T(8,128)S(1)} custom-call(bf16[128,4096]{1,0:T(8,128)(2,1)} %bitcast.7, bf16[128,7168]{1,0:T(8,128)(2,1)} %bitcast.6, bf16[64,4096]{1,0:T(8,128)(2,1)} %bitcast.9, bf16[64,7168]{1,0:T(8,128)(2,1)} %bitcast.8), custom_call_target="tpu_custom_call" | custom-call | tf_op jit(solution)/shard_map/project/pallas_call | solution.py:60
  3.2 0.5 %collective-permute-start = (f32[128,128]{1,0:T(8,128)S(1)}, f32[128,128]{1,0:T(8,128)S(1)}, u32[]{:S(2)}, u32[]{:S(2)}) collective-permute-start(f32[128,128]{1,0:T(8,128)S(1)} %project.1.mine), channel_id=1, source_target_pairs={{0,2},{2,0},{1,3},{3,1},{4,6},{6,4},{5,7},{7,5},{8,10},{10,8},{9,1... | collective-permute-start | bytes 196616 | tf_op jit(solution)/shard_map/ppermute | solution.py:274
  3.7 0.0 copy-done.1
  3.7 0.0 copy-done.2
  3.7 0.1 tags.1.marks
  3.8 0.8 %collective-permute-done.other = f32[128,128]{1,0:T(8,128)S(1)} collective-permute-done((f32[128,128]{1,0:T(8,128)S(1)}, f32[128,128]{1,0:T(8,128)S(1)}, u32[]{:S(2)}, u32[]{:S(2)}) %collective-permute-start) | collective-permute-done | bytes 65568 | tf_op jit(solution)/shard_map/ppermute | solution.py:274
  4.7 3.8 %collective-permute-start.1 = (f16[136,128]{1,0:T(8,128)(2,1)S(1)}, f16[136,128]{1,0:T(8,128)(2,1)S(1)}, u32[]{:S(2)}, u32[]{:S(2)}) collective-permute-start(f16[136,128]{1,0:T(8,128)(2,1)S(1)} %get-tuple-element.6), channel_id=1, source_target_pairs={{0,10},{2,12},{4,14},{6,8},{8,2},{10,4},{12,6},{14,0},{1,11},{3,13... | collective-permute-start | bytes 104456 | tf_op jit(solution)/shard_map/ppermute | solution.py:277
  8.4 1.4 %collective-permute-start.2 = (f16[136,128]{1,0:T(8,128)(2,1)S(1)}, f16[136,128]{1,0:T(8,128)(2,1)S(1)}, u32[]{:S(2)}, u32[]{:S(2)}) collective-permute-start(f16[136,128]{1,0:T(8,128)(2,1)S(1)} %get-tuple-element.6), channel_id=1, source_target_pairs={{2,4},{0,2},{6,0},{4,6},{10,12},{8,10},{14,8},{12,14},{3,5},{1,3},... | collective-permute-start | bytes 104456 | tf_op jit(solution)/shard_map/ppermute | solution.py:293
  9.8 0.0 copy-done
  9.8 0.3 %turn.1.train = bf16[4096,128]{1,0:T(8,128)(2,1)S(1)} custom-call(bf16[128,4096]{1,0:T(8,128)(2,1)S(1)} %bitcast.5), custom_call_target="tpu_custom_call" | custom-call | tf_op jit(solution)/shard_map/turn/pallas_call | solution.py:126
  10.2 1.0 %collective-permute-done.1 = f16[136,128]{1,0:T(8,128)(2,1)S(1)} collective-permute-done((f16[136,128]{1,0:T(8,128)(2,1)S(1)}, f16[136,128]{1,0:T(8,128)(2,1)S(1)}, u32[]{:S(2)}, u32[]{:S(2)}) %collective-permute-start.1) | collective-permute-done | bytes 34848 | tf_op jit(solution)/shard_map/ppermute | solution.py:277
  11.2 0.6 %far.1.first = f32[32,128]{1,0:T(8,128)S(1)} custom-call(f32[32,128]{1,0:T(8,128)S(1)} %own.1.scored, f32[136,128]{1,0:T(8,128)S(1)} %convert_element_type.14.far, bf16[4096,128]{1,0:T(8,128)(2,1)S(1)} %turn.1.train), custom_call_target="tpu_custom_call" | custom-call | tf_op jit(solution)/shard_map/far/pallas_call | solution.py:260
  11.8 0.0 collective-permute-done.2
  11.9 0.5 %collective-permute-start.3 = (f32[32,128]{1,0:T(8,128)S(1)}, f32[32,128]{1,0:T(8,128)S(1)}, u32[]{:S(2)}, u32[]{:S(2)}) collective-permute-start(f32[32,128]{1,0:T(8,128)S(1)} %sent.1), channel_id=1, source_target_pairs={{0,3},{2,1},{1,2},{3,0},{4,7},{6,5},{5,6},{7,4},{8,11},{10,9},{9,1... | collective-permute-start | bytes 49160 | tf_op jit(solution)/shard_map/ppermute | solution.py:284
  12.4 0.6 %kept.1 = f32[32,128]{1,0:T(8,128)S(1)} custom-call(f32[32,128]{1,0:T(8,128)S(1)} %own.1.scored, f32[136,128]{1,0:T(8,128)S(1)} %convert_element_type.14.far, f32[136,128]{1,0:T(8,128)S(1)} %convert_element_type.15.near, bf16[4096,128]{1,0:T(8,128)(2,1)S(1)} %turn.1.train), custom_call_target="tpu_custom_call" | custom-call | tf_op jit(solution)/shard_map/kept/pallas_call | solution.py:260
  13.0 2.1 %collective-permute-done.3 = f32[32,128]{1,0:T(8,128)S(1)} collective-permute-done((f32[32,128]{1,0:T(8,128)S(1)}, f32[32,128]{1,0:T(8,128)S(1)}, u32[]{:S(2)}, u32[]{:S(2)}) %collective-permute-start.3) | collective-permute-done | bytes 16416 | tf_op jit(solution)/shard_map/ppermute | solution.py:284
  15.1 0.4 %collective-permute-start.4 = (f32[64,128]{1,0:T(8,128)S(1)}, f32[64,128]{1,0:T(8,128)S(1)}, u32[]{:S(2)}, u32[]{:S(2)}) collective-permute-start(f32[64,128]{1,0:T(8,128)S(1)} %maximum_select_fusion), channel_id=1, source_target_pairs={{0,2},{2,0},{1,3},{3,1},{4,6},{6,4},{5,7},{7,5},{8,10},{10,8},{9,1... | collective-permute-start | bytes 98312 | tf_op jit(solution)/shard_map/ppermute | solution.py:274
  15.6 0.9 %collective-permute-done.4 = f32[64,128]{1,0:T(8,128)S(1)} collective-permute-done((f32[64,128]{1,0:T(8,128)S(1)}, f32[64,128]{1,0:T(8,128)S(1)}, u32[]{:S(2)}, u32[]{:S(2)}) %collective-permute-start.4) | collective-permute-done | bytes 32800 | tf_op jit(solution)/shard_map/ppermute | solution.py:274
  16.4 0.6 %add.12 = f32[64,128]{1,0:T(8,128)} add(f32[64,128]{1,0:T(8,128)S(1)} %maximum_select_fusion, f32[64,128]{1,0:T(8,128)S(1)} %collective-permute-done.4) | non-fusion elementwise | flops 8192 | bytes 98304 | tf_op jit(solution)/shard_map/add | solution.py:301
  (7 shorter events, 0.1 us)
Async XLA Ops:
  0.0 3.7 %copy-start.1 = (s32[1,32]{1,0:T(1,128)S(1)}, s32[1,32]{1,0:T(1,128)}, u32[]{:S(2)}) copy-start(s32[1,32]{1,0:T(1,128)} %lengths.1) | copy-start | bytes 388
  0.0 3.7 %copy-start.2 = (s32[1,32]{1,0:T(1,128)S(1)}, s32[1,32]{1,0:T(1,128)}, u32[]{:S(2)}) copy-start(s32[1,32]{1,0:T(1,128)} %query_ids.1) | copy-start | bytes 388
  0.0 9.8 %copy-start = (bf16[1,128,4096]{2,1,0:T(8,128)(2,1)S(1)}, bf16[1,128,4096]{2,1,0:T(8,128)(2,1)}, u32[]{:S(2)}) copy-start(bf16[1,128,4096]{2,1,0:T(8,128)(2,1)} %param.13) | copy-start | bytes 3145732
  3.2 1.4 %collective-permute-start = (f32[128,128]{1,0:T(8,128)S(1)}, f32[128,128]{1,0:T(8,128)S(1)}, u32[]{:S(2)}, u32[]{:S(2)}) collective-permute-start(f32[128,128]{1,0:T(8,128)S(1)} %project.1.mine), channel_id=1, source_target_pairs={{0,2},{2,0},{1,3},{3,1},{4,6},{6,4},{5,7},{7,5},{8,10},{10,8},{9,1... | collective-permute-start | bytes 196616 | tf_op jit(solution)/shard_map/ppermute | solution.py:274
  4.7 6.5 %collective-permute-start.1 = (f16[136,128]{1,0:T(8,128)(2,1)S(1)}, f16[136,128]{1,0:T(8,128)(2,1)S(1)}, u32[]{:S(2)}, u32[]{:S(2)}) collective-permute-start(f16[136,128]{1,0:T(8,128)(2,1)S(1)} %get-tuple-element.6), channel_id=1, source_target_pairs={{0,10},{2,12},{4,14},{6,8},{8,2},{10,4},{12,6},{14,0},{1,11},{3,13... | collective-permute-start | bytes 104456 | tf_op jit(solution)/shard_map/ppermute | solution.py:277
  8.4 3.4 %collective-permute-start.2 = (f16[136,128]{1,0:T(8,128)(2,1)S(1)}, f16[136,128]{1,0:T(8,128)(2,1)S(1)}, u32[]{:S(2)}, u32[]{:S(2)}) collective-permute-start(f16[136,128]{1,0:T(8,128)(2,1)S(1)} %get-tuple-element.6), channel_id=1, source_target_pairs={{2,4},{0,2},{6,0},{4,6},{10,12},{8,10},{14,8},{12,14},{3,5},{1,3},... | collective-permute-start | bytes 104456 | tf_op jit(solution)/shard_map/ppermute | solution.py:293
  11.9 3.2 %collective-permute-start.3 = (f32[32,128]{1,0:T(8,128)S(1)}, f32[32,128]{1,0:T(8,128)S(1)}, u32[]{:S(2)}, u32[]{:S(2)}) collective-permute-start(f32[32,128]{1,0:T(8,128)S(1)} %sent.1), channel_id=1, source_target_pairs={{0,3},{2,1},{1,2},{3,0},{4,7},{6,5},{5,6},{7,4},{8,11},{10,9},{9,1... | collective-permute-start | bytes 49160 | tf_op jit(solution)/shard_map/ppermute | solution.py:284
  15.1 1.3 %collective-permute-start.4 = (f32[64,128]{1,0:T(8,128)S(1)}, f32[64,128]{1,0:T(8,128)S(1)}, u32[]{:S(2)}, u32[]{:S(2)}) collective-permute-start(f32[64,128]{1,0:T(8,128)S(1)} %maximum_select_fusion), channel_id=1, source_target_pairs={{0,2},{2,0},{1,3},{3,1},{4,6},{6,4},{5,7},{7,5},{8,10},{10,8},{9,1... | collective-permute-start | bytes 98312 | tf_op jit(solution)/shard_map/ppermute | solution.py:274
